TPU v7x, 32 devices: a whole 2x2x4 slice. The times are simulated.
32 devices in a mesh: groups: 2 (over x), role: 2 (over core), seq: 8 (over z, y).
Axes of the slice: x: 2, y: 2, z: 4, core: 2. Of those that a mesh axis runs over, the one named last changes fastest.
Arguments:
- token_kv: bfloat16 [2, 8192, 2, 1024], P('role', ('groups', 'seq')), parts along dimension 1, may hold values from -6 to 6
- positions: int32 [2, 8192], P('role', ('groups', 'seq')), parts along dimension 1, may hold values from 0 to 131071, as said below
- page_owner: int32 [512], P(('groups', 'seq')), parts along dimension 0, may hold values from 0 to 7, as said below
- queries: bfloat16 [256, 8192], P('groups'), parts along dimension 0, may hold values from -220 to 220
- own_kv: bfloat16 [256, 2, 1024], P('groups'), parts along dimension 0, may hold values from -6 to 6
- selected: int32 [256, 8, 32], P('groups'), parts along dimension 0, may hold values from 0 to 1279, as said below
- lengths: int32 [256], P('groups'), parts along dimension 0, may hold values from 32768 to 131072
Outputs:
- attended: bfloat16 [256, 8192], P(('groups', 'role', 'seq')), parts along dimension 0
- bounds: float32 [256, 2048], P(('groups', 'role', 'seq')), parts along dimension 0
There are 2 independent parts, one for each index of `groups`. A program takes and returns all parts, laid end to end along the dimension named above; each array names one. Nothing has to cross between parts.
Inputs may be any that keep to these rules, and one draw needn't show every extreme that they name: `page_owner`: among the 32 pages of one prefill device no owner appears more than 16 times, and one owner takes exactly 16 pages of every prefill device. `selected`: the 32 numbers of one row and key head are distinct numbers of existing pages. Within the 512 tokens of one device positions rise by one from a multiple of 16.
All inputs are finite; a program needn't handle non-finite values.
Results may differ from a plain program's by a relative error of at most 0.0075.
Values may be sent and summed in bfloat16 or wider, within the bound.
A program may use at most 128 MiB of HBM per device.

v0:
```python
import math

import jax
import jax.numpy as jnp
from jax import lax
from jax.sharding import PartitionSpec as P

NEG = -1e30


def from_behind(block, axis, distance):
    devices = range(lax.axis_size(axis))
    route = [(i - distance, i) for i in devices if i - distance in devices]
    return lax.ppermute(block, axis, route)


def owner_rank(owners):
    page_total = owners.shape[0]
    same_owner = owners[:, None] == owners[None, :]
    earlier = jnp.arange(page_total)[None, :] < jnp.arange(page_total)[:, None]
    return jnp.sum(same_owner & earlier, axis=1)


def pack_pages(target, slot_total, flat_kv, flat_sum, page_pos):
    chosen = jnp.arange(slot_total, dtype=jnp.int32)[:, None] == target[None, :]
    onehot = chosen.astype(jnp.bfloat16)
    sent_kv = jnp.dot(onehot, flat_kv, preferred_element_type=jnp.float32).astype(jnp.bfloat16)
    sent_sum = jnp.dot(onehot, flat_sum, preferred_element_type=jnp.float32).astype(jnp.bfloat16)
    sent_pos = jnp.sum(jnp.where(chosen[:, :, None], page_pos[None], 0), axis=1)
    return (sent_kv, sent_sum, sent_pos)


def attend(pool_kv, pool_sum, pool_pos, pool_ids, queries, selected, lengths, kv_heads):
    pool_total, page_len = pool_pos.shape
    kv_width = pool_kv.shape[-1]
    head_dim = kv_width // kv_heads
    row_total = queries.shape[0]
    group_size = queries.shape[1] // kv_width
    score_scale = 1.0 / math.sqrt(head_dim)
    token_total = pool_total * page_len
    row_block = 32
    block_count = row_total // row_block
    key_heads = jnp.transpose(
        pool_kv[:, :, 0, :].reshape(token_total, kv_heads, head_dim), (1, 0, 2)
    )
    value_heads = jnp.transpose(
        pool_kv[:, :, 1, :].reshape(token_total, kv_heads, head_dim), (1, 0, 2)
    )
    summary_heads = jnp.transpose(pool_sum.reshape(pool_total, 2, kv_heads, head_dim), (2, 0, 1, 3))
    timely = (pool_pos[None] < lengths[:, None, None]).reshape(
        block_count, row_block, pool_total, page_len
    )
    query_heads = jnp.transpose(
        queries.reshape(row_total, kv_heads, group_size, head_dim), (1, 0, 2, 3)
    )
    chosen_heads = jnp.transpose(selected, (1, 0, 2))

    def one_head(inputs):
        key_rows, value_rows, summary, query_head, chosen = inputs
        query_blocks = query_head.reshape(block_count, row_block, group_size, head_dim)
        chosen_blocks = chosen.reshape(block_count, row_block, chosen.shape[-1])

        def one_block(parts):
            query_block, chosen_block, timely_block = parts
            matches = chosen_block[:, :, None] == pool_ids[None, None, :]
            picked = jnp.any(matches, axis=1)
            usable = (picked[:, :, None] & timely_block).reshape(row_block, token_total)
            scores = (
                jnp.einsum("rgd,td->rgt", query_block, key_rows, preferred_element_type=jnp.float32)
                * score_scale
            )
            masked = jnp.where(usable[:, None, :], scores, NEG)
            largest = jnp.max(masked, axis=2)
            weights = jnp.where(usable[:, None, :], jnp.exp(masked - largest[:, :, None]), 0.0)
            totals = jnp.sum(weights, axis=2)
            sums = jnp.einsum(
                "rgt,td->rgd",
                weights.astype(jnp.bfloat16),
                value_rows,
                preferred_element_type=jnp.float32,
            )
            upper_part = jnp.maximum(query_block, 0)
            lower_part = jnp.maximum(-query_block, 0)
            upper_bound = jnp.einsum(
                "rgd,qd->rgq", upper_part, summary[:, 0], preferred_element_type=jnp.float32
            )
            upper_bound = (
                upper_bound
                - jnp.einsum(
                    "rgd,qd->rgq", lower_part, summary[:, 1], preferred_element_type=jnp.float32
                )
            ) * score_scale
            bound = jnp.einsum(
                "mfp,mlp->mlf",
                matches.astype(jnp.float32),
                upper_bound,
                precision=lax.Precision.HIGHEST,
            )
            return (largest, totals, sums, bound)

        largest, totals, sums, bound = lax.map(one_block, (query_blocks, chosen_blocks, timely))
        return (
            largest.reshape(row_total, group_size),
            totals.reshape(row_total, group_size),
            sums.reshape(row_total, group_size, head_dim),
            bound.reshape(row_total, group_size, -1),
        )

    largest, totals, sums, bounds = lax.map(
        one_head, (key_heads, value_heads, summary_heads, query_heads, chosen_heads)
    )
    largest = jnp.transpose(largest, (1, 0, 2)).reshape(row_total, kv_heads * group_size)
    totals = jnp.transpose(totals, (1, 0, 2)).reshape(row_total, kv_heads * group_size)
    sums = jnp.transpose(sums, (1, 0, 2, 3)).reshape(row_total, kv_heads * group_size, head_dim)
    bounds = jnp.transpose(bounds, (1, 0, 2, 3)).reshape(row_total, kv_heads * group_size, -1)
    return (largest, totals, sums, bounds)


def body(token_kv, positions, page_owner, queries, own_kv, selected, lengths):
    seq_total = lax.axis_size("seq")
    role_index = lax.axis_index("role")
    seq_index = lax.axis_index("seq")
    decoding = role_index == 1
    page_dev = page_owner.shape[0]
    tokens_dev = token_kv.shape[1]
    kv_width = token_kv.shape[3]
    page_len = tokens_dev // page_dev
    kv_heads = selected.shape[1]
    slot_count = max(2, 4 * page_dev // seq_total)
    inbound = seq_total * slot_count
    pool_dev = inbound + page_dev
    local_kv = token_kv[0].reshape(page_dev, page_len, 2, kv_width)
    local_pos = positions[0].reshape(page_dev, page_len)
    local_keys = local_kv[:, :, 0, :]
    local_sum = jnp.stack([jnp.max(local_keys, axis=1), jnp.min(local_keys, axis=1)], axis=1)
    order_rank = owner_rank(page_owner)
    flat_kv = local_kv.reshape(page_dev, page_len * 2 * kv_width)
    flat_sum = local_sum.reshape(page_dev, 2 * kv_width)
    out_kv, out_sum, out_pos = pack_pages(
        page_owner * slot_count + order_rank, inbound, flat_kv, flat_sum, local_pos
    )
    routed_kv, routed_sum, routed_pos = (
        lax.all_to_all(out_kv, "seq", split_axis=0, concat_axis=0, tiled=True),
        lax.all_to_all(out_sum, "seq", split_axis=0, concat_axis=0, tiled=True),
        lax.all_to_all(out_pos, "seq", split_axis=0, concat_axis=0, tiled=True),
    )
    got_kv, got_sum, got_pos = from_behind((routed_kv, routed_sum, routed_pos), "role", 1)
    pool_kv = jnp.concatenate([got_kv.reshape(inbound, page_len, 2, kv_width), local_kv], axis=0)
    pool_sum = jnp.concatenate([got_sum.reshape(inbound, 2, kv_width), local_sum], axis=0)
    pool_pos = jnp.concatenate([got_pos, local_pos], axis=0)
    pool_ids = jnp.where(decoding, seq_index * pool_dev + jnp.arange(pool_dev, dtype=jnp.int32), -1)
    largest, totals, sums, bounds = attend(
        pool_kv, pool_sum, pool_pos, pool_ids, queries, selected, lengths, kv_heads
    )
    row_total = queries.shape[0]
    device_total = 2 * seq_total
    rows_here = row_total // device_total
    first_row = (role_index * seq_total + seq_index) * rows_here
    overall = lax.pmax(largest, ("role", "seq"))
    factor = jnp.exp(largest - overall)
    sums, totals, bounds = (
        lax.psum_scatter(
            sums * factor[..., None], ("role", "seq"), scatter_dimension=0, tiled=True
        ),
        lax.psum_scatter(totals * factor, ("role", "seq"), scatter_dimension=0, tiled=True),
        lax.psum_scatter(bounds, ("role", "seq"), scatter_dimension=0, tiled=True),
    )
    largest = lax.dynamic_slice_in_dim(overall, first_row, rows_here, 0)
    head_dim = kv_width // kv_heads
    group_size = queries.shape[1] // kv_width
    score_scale = 1.0 / math.sqrt(head_dim)
    my_queries = lax.dynamic_slice_in_dim(queries, first_row, rows_here, 0).reshape(
        rows_here, kv_heads, group_size, head_dim
    )
    my_own = lax.dynamic_slice_in_dim(own_kv, first_row, rows_here, 0)
    own_keys = my_own[:, 0].reshape(rows_here, kv_heads, head_dim)
    own_values = my_own[:, 1].reshape(rows_here, kv_heads, 1, head_dim).astype(jnp.float32)
    own_score = (
        jnp.einsum(
            "rhgd,rhd->rhg", my_queries, own_keys, preferred_element_type=jnp.float32
        ).reshape(rows_here, kv_heads * group_size)
        * score_scale
    )
    highest = jnp.maximum(largest, own_score)
    fading = jnp.exp(largest - highest)
    fresh_weight = jnp.exp(own_score - highest)
    value_share = jnp.broadcast_to(own_values, (rows_here, kv_heads, group_size, head_dim)).reshape(
        rows_here, kv_heads * group_size, head_dim
    )
    attended = (sums * fading[..., None] + fresh_weight[..., None] * value_share) / (
        totals * fading + fresh_weight
    )[..., None]
    return (attended.reshape(rows_here, -1).astype(jnp.bfloat16), bounds.reshape(rows_here, -1))


def solution(mesh):
    in_specs = (
        P("role", ("groups", "seq"), None, None),
        P("role", ("groups", "seq")),
        P(("groups", "seq")),
        P("groups", None),
        P("groups", None, None),
        P("groups", None, None),
        P("groups"),
    )
    out_specs = (P(("groups", "role", "seq"), None), P(("groups", "role", "seq"), None))
    return jax.shard_map(body, mesh=mesh, in_specs=in_specs, out_specs=out_specs, check_vma=False)
```

profile of v0, /device:TPU:0, one launch (start us, length us, event | category | flops | bytes accessed | tf_op | source)
XLA Modules:
  0.0 771.3 jit_solution(9747603946659386819)
XLA Ops:
  14.5 190.4 %all_to_all.36 = bf16[8,16,32768]{2,1,0:T(8,128)(2,1)} all-to-all(bf16[8,16,32768]{2,1,0:T(8,128)(2,1)S(1)} %bitcast.187), channel_id=1, replica_groups=mesh['groups'=2,'role'=2,'seq'=8] {'seq'}, dimensions={0} | all-to-all | bytes 16777216 | tf_op jit(solution)/shard_map/all_to_all | solution.py:143
  204.9 4.6 collective-permute-start
  211.1 14.3 %all_to_all.37 = bf16[8,16,2048]{2,1,0:T(8,128)(2,1)S(1)} all-to-all(bf16[8,16,2048]{2,1,0:T(8,128)(2,1)S(1)} %bitcast.198), channel_id=1, replica_groups=mesh['groups'=2,'role'=2,'seq'=8] {'seq'}, dimensions={0} | all-to-all | bytes 1048576 | tf_op jit(solution)/shard_map/all_to_all | solution.py:144
  229.2 9.9 %all_to_all.38 = s32[8,1,256]{2,1,0:T(1,128)S(1)} all-to-all(s32[8,1,256]{2,1,0:T(1,128)S(1)} %reshape.160), channel_id=1, replica_groups=mesh['groups'=2,'role'=2,'seq'=8] {'seq'}, dimensions={0} | all-to-all | bytes 16384 | tf_op jit(solution)/shard_map/all_to_all | solution.py:145
  242.4 6.1 copy.249
  248.6 4.1 copy.245
  256.7 11.9 %copy.247 = bf16[128,32768]{0,1:T(8,128)(2,1)} copy(bf16[128,32768]{1,0:T(8,128)(2,1)} %collective-permute-done) | data formatting | bytes 16777216 | tf_op jit(solution)/shard_map/ppermute | solution.py:14
  268.6 12.4 %pad_maximum_fusion = (bf16[160,16,1,1024]{0,3,2,1:T(8,128)(2,1)}, bf16[160,16,1,1024]{0,3,2,1:T(8,128)(2,1)}) fusion(bf16[32,16,2,1024]{0,3,2,1:T(8,128)(2,1)} %copy.249, bf16[128,16,2,1024]{0,3,2,1:T(8,128)(2,1)} %bitcast.188), kind=kLoop, calls=%fused_computation.66 | loop fusion | flops 20971520 | bytes 20971520 | tf_op jit(solution)/shard_map/concatenate | solution.py:148
  281.0 11.8 %copy.250 = bf16[160,16,1,1024]{3,1,0,2:T(8,128)(2,1)} copy(bf16[160,16,1,1024]{0,3,2,1:T(8,128)(2,1)} %get-tuple-element.429) | data formatting | bytes 10485760 | tf_op jit(solution)/shard_map/slice | solution.py:44
  299.8 11.8 %copy.251 = bf16[160,16,1,1024]{3,1,0,2:T(8,128)(2,1)} copy(bf16[160,16,1,1024]{0,3,2,1:T(8,128)(2,1)} %get-tuple-element.428) | data formatting | bytes 10485760 | tf_op jit(solution)/shard_map/slice | solution.py:47
  318.7 304.0 %while.35 = (s32[]{:T(128)}, f32[8,128,8]{1,2,0:T(8,128)}, f32[8,128,8]{1,2,0:T(8,128)}, f32[8,128,8,128]{3,2,0,1:T(8,128)}, f32[8,128,8,32]{1,3,2,0:T(8,128)}, ...) while((s32[]{:T(128)}, f32[8,128,8]{1,2,0:T(8,128)}, ...), condition=%wide.region_10.11_spmd.clone, body=%wide.region_4.10_spmd.clone.sunk | while | flops 379218752 | bytes 17099060 | solution.py:109
  323.9 26.0 %while.36 = (s32[]{:T(128)}, f32[4,32,8]{2,1,0:T(8,128)}, f32[4,32,8]{2,1,0:T(8,128)}, f32[4,32,8,128]{3,2,1,0:T(8,128)}, f32[4,32,8,32]{3,2,1,0:T(8,128)}, /*in...) while((s32[]{:T(128)}, f32[4,32,8]{2,1,0:T(8,128)}, ...), condition=%wide.region_9.9_spmd, body=%wide.region_5.8_spmd.sunk | while | flops 378890752 | bytes 11285393 | solution.py:101
  361.9 26.0 %while.36 = (s32[]{:T(128)}, f32[4,32,8]{2,1,0:T(8,128)}, f32[4,32,8]{2,1,0:T(8,128)}, f32[4,32,8,128]{3,2,1,0:T(8,128)}, f32[4,32,8,32]{3,2,1,0:T(8,128)}, /*in...) while((s32[]{:T(128)}, f32[4,32,8]{2,1,0:T(8,128)}, ...), condition=%wide.region_9.9_spmd, body=%wide.region_5.8_spmd.sunk | while | flops 378890752 | bytes 11285393 | solution.py:101
  399.9 26.0 %while.36 = (s32[]{:T(128)}, f32[4,32,8]{2,1,0:T(8,128)}, f32[4,32,8]{2,1,0:T(8,128)}, f32[4,32,8,128]{3,2,1,0:T(8,128)}, f32[4,32,8,32]{3,2,1,0:T(8,128)}, /*in...) while((s32[]{:T(128)}, f32[4,32,8]{2,1,0:T(8,128)}, ...), condition=%wide.region_9.9_spmd, body=%wide.region_5.8_spmd.sunk | while | flops 378890752 | bytes 11285393 | solution.py:101
  437.9 26.0 %while.36 = (s32[]{:T(128)}, f32[4,32,8]{2,1,0:T(8,128)}, f32[4,32,8]{2,1,0:T(8,128)}, f32[4,32,8,128]{3,2,1,0:T(8,128)}, f32[4,32,8,32]{3,2,1,0:T(8,128)}, /*in...) while((s32[]{:T(128)}, f32[4,32,8]{2,1,0:T(8,128)}, ...), condition=%wide.region_9.9_spmd, body=%wide.region_5.8_spmd.sunk | while | flops 378890752 | bytes 11285393 | solution.py:101
  475.9 26.0 %while.36 = (s32[]{:T(128)}, f32[4,32,8]{2,1,0:T(8,128)}, f32[4,32,8]{2,1,0:T(8,128)}, f32[4,32,8,128]{3,2,1,0:T(8,128)}, f32[4,32,8,32]{3,2,1,0:T(8,128)}, /*in...) while((s32[]{:T(128)}, f32[4,32,8]{2,1,0:T(8,128)}, ...), condition=%wide.region_9.9_spmd, body=%wide.region_5.8_spmd.sunk | while | flops 378890752 | bytes 11285393 | solution.py:101
  513.9 26.0 %while.36 = (s32[]{:T(128)}, f32[4,32,8]{2,1,0:T(8,128)}, f32[4,32,8]{2,1,0:T(8,128)}, f32[4,32,8,128]{3,2,1,0:T(8,128)}, f32[4,32,8,32]{3,2,1,0:T(8,128)}, /*in...) while((s32[]{:T(128)}, f32[4,32,8]{2,1,0:T(8,128)}, ...), condition=%wide.region_9.9_spmd, body=%wide.region_5.8_spmd.sunk | while | flops 378890752 | bytes 11285393 | solution.py:101
  551.9 26.0 %while.36 = (s32[]{:T(128)}, f32[4,32,8]{2,1,0:T(8,128)}, f32[4,32,8]{2,1,0:T(8,128)}, f32[4,32,8,128]{3,2,1,0:T(8,128)}, f32[4,32,8,32]{3,2,1,0:T(8,128)}, /*in...) while((s32[]{:T(128)}, f32[4,32,8]{2,1,0:T(8,128)}, ...), condition=%wide.region_9.9_spmd, body=%wide.region_5.8_spmd.sunk | while | flops 378890752 | bytes 11285393 | solution.py:101
  589.9 26.0 %while.36 = (s32[]{:T(128)}, f32[4,32,8]{2,1,0:T(8,128)}, f32[4,32,8]{2,1,0:T(8,128)}, f32[4,32,8,128]{3,2,1,0:T(8,128)}, f32[4,32,8,32]{3,2,1,0:T(8,128)}, /*in...) while((s32[]{:T(128)}, f32[4,32,8]{2,1,0:T(8,128)}, ...), condition=%wide.region_9.9_spmd, body=%wide.region_5.8_spmd.sunk | while | flops 378890752 | bytes 11285393 | solution.py:101
  622.7 4.1 copy.273
  627.1 58.3 %pmax.7 = f32[128,64]{1,0:T(8,128)S(1)} all-reduce(f32[128,64]{1,0:T(8,128)S(1)} %copy.267), channel_id=1, replica_groups=mesh['groups'=2,'role'=2,'seq'=8] {'role','seq'}, use_global_device_ids=true, to_apply=%region_11.12 | all-reduce | flops 8192 | bytes 65536 | tf_op jit(solution)/shard_map/pmax | solution.py:159
  685.4 4.2 bitcast_multiply_fusion
  693.7 58.6 %all-reduce = f32[128,64]{0,1:T(8,128)S(1)} all-reduce(f32[128,64]{0,1:T(8,128)S(1)} %copy.270), channel_id=3, replica_groups=mesh['groups'=2,'role'=2,'seq'=8] {'role','seq'}, use_global_device_ids=true, to_apply=%region_13.14.clone | all-reduce | flops 8192 | bytes 65536
  754.3 8.2 %reduce-scatter.4.cloned.1.call-done = f32[8,64,128]{2,1,0:T(8,128)} async-done(((f32[128,64,128]{2,1,0:T(8,128)}), f32[8,64,128]{2,1,0:T(8,128)}) %reduce-scatter.4.cloned.1.call-update) | async-done | bytes 262160 | tf_op jit(solution)/shard_map/reduce_scatter | solution.py:162
  (641 shorter events, 343.5 us)
Async XLA Ops:
  7.2 745.3 %reduce-scatter.6.cloned.1.call-start = ((), (), s32[]{:S(2)}) async-start(), calls=%async_computation.6 | async-start | bytes 2228224 | tf_op jit(solution)/shard_map/reduce_scatter | solution.py:166
  14.5 195.0 %copy-start = (bf16[1,512,2,1024]{3,2,1,0:T(2,128)(2,1)S(1)}, bf16[1,512,2,1024]{3,2,1,0:T(2,128)(2,1)}, u32[]{:S(2)}) copy-start(bf16[1,512,2,1024]{3,2,1,0:T(2,128)(2,1)} %param.11) | copy-start | bytes 6291460
  204.9 23.1 %copy-start.4 = (s32[1,512]{1,0:T(1,128)S(1)}, s32[1,512]{1,0:T(1,128)}, u32[]{:S(2)}) copy-start(s32[1,512]{1,0:T(1,128)} %param.12) | copy-start | bytes 6148
  204.9 51.7 %collective-permute-start = (bf16[128,32768]{1,0:T(8,128)(2,1)}, bf16[128,32768]{1,0:T(8,128)(2,1)}, u32[]{:S(2)}, u32[]{:S(2)}) collective-permute-start(bf16[128,32768]{1,0:T(8,128)(2,1)} %bitcast.20), channel_id=1, source_target_pairs={{0,8},{1,9},{2,10},{3,11},{4,12},{5,13},{6,14},{7,15},{16,24},{17,... | collective-permute-start | bytes 25165832 | tf_op jit(solution)/shard_map/ppermute | solution.py:14
  225.5 28.4 %collective-permute-start.1 = (bf16[128,2048]{1,0:T(8,128)(2,1)S(1)}, bf16[128,2048]{1,0:T(8,128)(2,1)}, u32[]{:S(2)}, u32[]{:S(2)}) collective-permute-start(bf16[128,2048]{1,0:T(8,128)(2,1)S(1)} %bitcast.207), channel_id=1, source_target_pairs={{0,8},{1,9},{2,10},{3,11},{4,12},{5,13},{6,14},{7,15},{16,24},{17,... | collective-permute-start | bytes 1572872 | tf_op jit(solution)/shard_map/ppermute | solution.py:14
  240.6 13.2 %collective-permute-start.2 = (s32[128,16]{0,1:T(8,128)S(1)}, s32[128,16]{0,1:T(8,128)S(1)}, u32[]{:S(2)}, u32[]{:S(2)}) collective-permute-start(s32[128,16]{0,1:T(8,128)S(1)} %all_to_all.32), channel_id=1, source_target_pairs={{0,8},{1,9},{2,10},{3,11},{4,12},{5,13},{6,14},{7,15},{16,24},{17,... | collective-permute-start | bytes 24584 | tf_op jit(solution)/shard_map/ppermute | solution.py:14
  248.5 4.1 copy-start.1
  248.5 5.1 copy-start.5
  622.7 4.1 copy-start.2
  622.7 4.3 copy-start.3
  626.8 135.7 %reduce-scatter.4.cloned.1.call-start = ((), (), s32[]{:S(2)}) async-start(), calls=%async_computation.5 | async-start | bytes 4456448 | tf_op jit(solution)/shard_map/reduce_scatter | solution.py:162
  689.6 2.0 copy-start.6
Sparse Core Ops, SparseCore 0:
  626.9 59.0 reduce-scatter.5
  690.4 72.0 reduce-scatter.3
where the time goes:
time: 776 us; the launch traced here: 771 us
  blocking collectives  332 us (43%)
  local copies, waits for them, and re-layouts  207 us (27%)
  matrix products  127 us (16%)
  other arithmetic  71.8 us (9%)
  between operations  15 us (2%)
  waiting for transfers between devices  8.25 us (1%)
  starting transfers between devices  8.24 us (1%)
    all_to_all x1, blocking collectives, body(): lax.all_to_all(out_kv, 'seq', split_axis=0, concat_axis=0, tiled=True)  190 us
    unnamed x1, blocking collectives  58.6 us
    pmax x1, blocking collectives, body(): overall = lax.pmax(largest, ('role', 'seq'))  58.3 us
    dynamic_update_slice x56, local copies, waits for them, and re-layouts, attend(): lax.map(one_head, (key_heads, value_heads, summary_heads, query_heads, ch...  54.4 us
    dot_general x32, matrix products, one_block(): jnp.einsum('rgt,td->rgd', weights.astype(jnp.bfloat16), value_rows, prefe...  42.8 us
    dot_general x32, matrix products, one_block(): jnp.einsum('mfp,mlp->mlf', matches.astype(jnp.float32), upper_bound, prec...  42.1 us
    dot_general x32, matrix products, one_block(): jnp.einsum('rgd,td->rgt', query_block, key_rows, preferred_element_type=j...  26 us
    reduce_sum x32, other arithmetic, one_block(): totals = jnp.sum(weights, axis=2)  25.2 us
  transfers between devices with their start and end apart: 5, of which 1 were waited for; matrix products, arithmetic and copies ran while one was open for 4% of the time, Pallas kernels for 0%

commit v1 on v0

--- a/solution.py
+++ b/solution.py
@@ -1,11 +1,16 @@
+import functools
 import math
 
 import jax
 import jax.numpy as jnp
 from jax import lax
+from jax.experimental import pallas as pl
+from jax.experimental.pallas import tpu as pltpu
 from jax.sharding import PartitionSpec as P
 
 NEG = -1e30
+LOG2E = 1.4426950408889634
+MESH = pl.DeviceIdType.MESH
 
 
 def from_behind(block, axis, distance):
@@ -193,6 +198,398 @@
     return (attended.reshape(rows_here, -1).astype(jnp.bfloat16), bounds.reshape(rows_here, -1))
 
 
+def exchange_kernel(
+    n_seq,
+    heads,
+    group,
+    scale,
+    ids_ref,
+    lens_ref,
+    pos_ref,
+    sel_ref,
+    own_ref,
+    ownv_ref,
+    q_hbm,
+    kv_hbm,
+    att_ref,
+    bnd_ref,
+    q_buf,
+    kv_own,
+    kv_got,
+    pos_got,
+    vt_buf,
+    s_buf,
+    p_buf,
+    bias_buf,
+    u_buf,
+    mt_buf,
+    lt_buf,
+    send_buf,
+    recv_buf,
+    ml_send,
+    ml_recv,
+    load_sem,
+    kv_send,
+    kv_recv,
+    o_send,
+    o_recv,
+):
+    role = lax.axis_index("role")
+    seq = lax.axis_index("seq")
+    n_dev = 2 * n_seq
+    me = role * n_seq + seq
+    mate = {"role": 1 - role, "seq": seq}
+    toks = kv_own.shape[1]
+    hd = kv_own.shape[2] // 2
+    pages = toks // 16
+    rows = q_buf.shape[0]
+    here = rows // n_dev
+    half = q_buf.shape[1]
+
+    q_copy = pltpu.make_async_copy(
+        q_hbm.at[:, pl.ds(pl.multiple_of(role * half, half), half)], q_buf, load_sem.at[0]
+    )
+    q_copy.start()
+    own_copy = pltpu.make_async_copy(kv_hbm.at[role], kv_own, load_sem.at[1])
+    own_copy.start()
+
+    barrier = pltpu.get_barrier_semaphore()
+
+    def greet(j, carry):
+        t = lax.rem(me + j, n_dev)
+        pl.semaphore_signal(
+            barrier, inc=1, device_id={"role": t // n_seq, "seq": t % n_seq}, device_id_type=MESH
+        )
+        return carry
+
+    lax.fori_loop(1, n_dev, greet, 0)
+    pl.semaphore_wait(barrier, n_dev - 1)
+
+    def mate_copy(hl):
+        return pltpu.make_async_remote_copy(
+            src_ref=kv_hbm.at[1 - role, hl],
+            dst_ref=kv_got.at[hl],
+            send_sem=kv_send.at[hl],
+            recv_sem=kv_recv.at[hl],
+            device_id=mate,
+            device_id_type=MESH,
+        )
+
+    pos_copy = pltpu.make_async_remote_copy(
+        src_ref=pos_ref,
+        dst_ref=pos_got,
+        send_sem=kv_send.at[heads],
+        recv_sem=kv_recv.at[heads],
+        device_id=mate,
+        device_id_type=MESH,
+    )
+    pos_copy.start()
+    for hl in range(heads):
+        mate_copy(hl).start()
+    q_copy.wait()
+    own_copy.wait()
+    pos_copy.wait()
+
+    mt_buf[...] = jnp.zeros_like(mt_buf)
+    lt_buf[...] = jnp.zeros_like(lt_buf)
+
+    def out_copy(hl, j):
+        t = lax.rem(me + j, n_dev)
+        return pltpu.make_async_remote_copy(
+            src_ref=send_buf.at[hl, t],
+            dst_ref=recv_buf.at[hl, me],
+            send_sem=o_send.at[hl, t],
+            recv_sem=o_recv.at[hl, me],
+            device_id={"role": t // n_seq, "seq": t % n_seq},
+            device_id_type=MESH,
+        )
+
+    def in_copy(hl, j):
+        t = lax.rem(me + j, n_dev)
+        return pltpu.make_async_remote_copy(
+            src_ref=send_buf.at[hl, t],
+            dst_ref=recv_buf.at[hl, t],
+            send_sem=o_send.at[hl, t],
+            recv_sem=o_recv.at[hl, t],
+            device_id={"role": t // n_seq, "seq": t % n_seq},
+            device_id_type=MESH,
+        )
+
+    def ml_out(j):
+        t = lax.rem(me + j, n_dev)
+        return pltpu.make_async_remote_copy(
+            src_ref=ml_send.at[t],
+            dst_ref=ml_recv.at[me],
+            send_sem=o_send.at[heads, t],
+            recv_sem=o_recv.at[heads, me],
+            device_id={"role": t // n_seq, "seq": t % n_seq},
+            device_id_type=MESH,
+        )
+
+    def ml_in(j):
+        t = lax.rem(me + j, n_dev)
+        return pltpu.make_async_remote_copy(
+            src_ref=ml_send.at[t],
+            dst_ref=ml_recv.at[t],
+            send_sem=o_send.at[heads, t],
+            recv_sem=o_recv.at[heads, t],
+            device_id={"role": t // n_seq, "seq": t % n_seq},
+            device_id_type=MESH,
+        )
+
+    lens = lens_ref[...]
+    n_sel = sel_ref.shape[1]
+    dims = (((1,), (1,)), ((), ()))
+
+    def one_head(hl, carry):
+        mate_copy(hl).wait()
+        sel = sel_ref[role * heads + hl]
+        ids = ids_ref[...]
+        hit = jnp.zeros((2 * pages, rows), jnp.float32) + NEG
+        for s in range(n_sel):
+            hit = jnp.where(ids == sel[s : s + 1, :], 0.0, hit)
+        for part in range(2):
+            start = (pos_ref if part == 0 else pos_got)[0:1, :]
+            left = lens - start
+            wide = jnp.broadcast_to(
+                hit[part * pages : (part + 1) * pages][:, None, :], (pages, 16, rows)
+            ).reshape(toks, rows)
+            place = lax.broadcasted_iota(jnp.int32, (toks, rows), 0)
+            bias_buf[part * toks : (part + 1) * toks, :] = jnp.where(place < left, wide, NEG)
+
+        tops = []
+        lows = []
+        for part in range(2):
+            block = kv_own if part == 0 else kv_got
+            k32 = block[hl, :, 0:hd].astype(jnp.float32).reshape(pages, 16, hd)
+            tops.append(jnp.max(k32, axis=1))
+            lows.append(jnp.min(k32, axis=1))
+            v32 = block[hl, :, hd : 2 * hd].astype(jnp.float32)
+            vt_buf[:, part * toks : (part + 1) * toks] = v32.T.astype(jnp.bfloat16)
+        summary = jnp.concatenate(
+            [jnp.concatenate(tops, axis=0), jnp.concatenate(lows, axis=0)], axis=1
+        ).astype(jnp.bfloat16)
+
+        def one_pair(gp, carry):
+            outs = []
+            for sub in range(2):
+                g = gp * 2 + sub
+                q = q_buf[:, pl.ds(pl.multiple_of((hl * group + g) * hd, hd), hd)]
+                q32 = q.astype(jnp.float32)
+                signed = jnp.concatenate(
+                    [jnp.maximum(q32, 0.0), jnp.minimum(q32, 0.0)], axis=1
+                ).astype(jnp.bfloat16)
+                u_buf[g] = (
+                    lax.dot_general(summary, signed, dims, preferred_element_type=jnp.float32)
+                    * scale
+                )
+                for part in range(2):
+                    block = kv_own if part == 0 else kv_got
+                    s_buf[sub, part * toks : (part + 1) * toks, :] = (
+                        lax.dot_general(
+                            block[hl, :, 0:hd], q, dims, preferred_element_type=jnp.float32
+                        )
+                        * (scale * LOG2E)
+                        + bias_buf[part * toks : (part + 1) * toks, :]
+                    )
+                top = jnp.max(s_buf[sub], axis=0, keepdims=True)
+                w = jnp.exp2(s_buf[sub] - top)
+                total = jnp.sum(w, axis=0, keepdims=True)
+                p_buf[sub] = w.astype(jnp.bfloat16)
+                o = jnp.dot(vt_buf[...], p_buf[sub], preferred_element_type=jnp.float32)
+                o = o * (1.0 / total)
+                mt_buf[pl.ds(hl * group + g, 1), :] = top
+                lt_buf[pl.ds(hl * group + g, 1), :] = total
+                outs.append(o.T.reshape(n_dev, here, hd))
+            send_buf[hl, :, pl.ds(pl.multiple_of(gp * 2 * here, 2 * here), 2 * here), :] = (
+                jnp.concatenate(outs, axis=1).astype(jnp.bfloat16)
+            )
+            return carry
+
+        lax.fori_loop(0, group // 2, one_pair, 0)
+
+        acc = [jnp.zeros((n_sel, rows), jnp.float32) for _ in range(group)]
+        for p in range(2 * pages):
+            same = sel == ids_ref[p : p + 1, :]
+            for g in range(group):
+                acc[g] = jnp.where(same, u_buf[g, p : p + 1, :], acc[g])
+        gs = group // 2
+        lefth = jnp.concatenate(acc[:gs], axis=0).T.reshape(n_dev, here, gs * n_sel)
+        righth = jnp.concatenate(acc[gs:], axis=0).T.reshape(n_dev, here, gs * n_sel)
+        send_buf[hl, :, group * here : group * here + 2 * here, :] = jnp.concatenate(
+            [lefth, righth], axis=1
+        ).astype(jnp.bfloat16)
+
+        def go(j, carry):
+            out_copy(hl, j).start()
+            return carry
+
+        lax.fori_loop(1, n_dev, go, 0)
+        recv_buf[hl, me] = send_buf[hl, me]
+        return carry
+
+    lax.fori_loop(0, heads, one_head, 0)
+
+    ml_send[:, 0:here, :] = mt_buf[...].T.reshape(n_dev, here, hd)
+    ml_send[:, here : 2 * here, :] = lt_buf[...].T.reshape(n_dev, here, hd)
+
+    def go_ml(j, carry):
+        ml_out(j).start()
+        return carry
+
+    lax.fori_loop(1, n_dev, go_ml, 0)
+    ml_recv[me] = ml_send[me]
+
+    def end_ml(j, carry):
+        ml_in(j).wait()
+        return carry
+
+    lax.fori_loop(1, n_dev, end_ml, 0)
+
+    shares = []
+    for r in range(2):
+        mine = own_ref[r]
+        tops = [ml_recv[r * n_seq + c, 0:here, :] for c in range(n_seq)]
+        highest = mine
+        for m in tops:
+            highest = jnp.maximum(highest, m)
+        fresh = jnp.exp2(mine - highest)
+        parts = [
+            jnp.exp2(tops[c] - highest) * ml_recv[r * n_seq + c, here : 2 * here, :]
+            for c in range(n_seq)
+        ]
+        inv = fresh
+        for w in parts:
+            inv = inv + w
+        inv = 1.0 / inv
+        shares.append([w * inv for w in parts] + [fresh * inv])
+
+    for hl in range(heads):
+
+        def end(j, carry):
+            in_copy(hl, j).wait()
+            return carry
+
+        lax.fori_loop(1, n_dev, end, 0)
+        for r in range(2):
+            h = r * heads + hl
+            own_v = ownv_ref[:, h * hd : (h + 1) * hd]
+            own_v = jnp.concatenate([own_v, own_v], axis=0)
+            for gp in range(group // 2):
+                j = hl * group + gp * 2
+
+                def column(w):
+                    return jnp.concatenate([w[:, j : j + 1], w[:, j + 1 : j + 2]], axis=0)
+
+                total = column(shares[r][n_seq]) * own_v
+                for c in range(n_seq):
+                    block = recv_buf[
+                        hl, r * n_seq + c, gp * 2 * here : (gp + 1) * 2 * here, :
+                    ].astype(jnp.float32)
+                    total = total + column(shares[r][c]) * block
+                at = (h * group + gp * 2) * hd
+                att_ref[:, at : at + hd] = total[0:here].astype(jnp.bfloat16)
+                att_ref[:, at + hd : at + 2 * hd] = total[here : 2 * here].astype(jnp.bfloat16)
+            bound = jnp.zeros((2 * here, hd), jnp.float32)
+            for c in range(n_seq):
+                bound = bound + recv_buf[
+                    hl, r * n_seq + c, group * here : (group + 2) * here, :
+                ].astype(jnp.float32)
+            at = h * group * n_sel
+            bnd_ref[:, at : at + hd] = bound[0:here]
+            bnd_ref[:, at + hd : at + 2 * hd] = bound[here : 2 * here]
+
+
+def direct_body(token_kv, positions, page_owner, queries, own_kv, selected, lengths):
+    seq_total = lax.axis_size("seq")
+    role_index = lax.axis_index("role")
+    seq_index = lax.axis_index("seq")
+    page_dev = page_owner.shape[0]
+    toks = token_kv.shape[1]
+    kv_width = token_kv.shape[3]
+    rows, kv_heads, n_sel = selected.shape
+    hd = kv_width // kv_heads
+    group = queries.shape[1] // kv_width
+    heads = kv_heads // 2
+    scale = 1.0 / math.sqrt(hd)
+    slot_count = max(2, 4 * page_dev // seq_total)
+    inbound = seq_total * slot_count
+    pool_dev = inbound + page_dev
+    n_dev = 2 * seq_total
+    here = rows // n_dev
+    me = role_index * seq_total + seq_index
+
+    new_ids = page_owner * pool_dev + seq_index * slot_count + owner_rank(page_owner)
+    old_ids = seq_index * pool_dev + inbound + jnp.arange(page_dev, dtype=jnp.int32)
+    ids = jnp.where(
+        role_index == 0,
+        jnp.concatenate([new_ids, old_ids]),
+        jnp.concatenate([old_ids, new_ids]),
+    )
+    ids = jnp.broadcast_to(ids[:, None], (2 * page_dev, rows)).astype(jnp.int32)
+    pos = jnp.broadcast_to(positions[:, 0:1], (8, rows))
+    sel = jnp.transpose(selected, (1, 2, 0))
+    kv = jnp.transpose(token_kv[0].reshape(toks, 2, 2, heads, hd), (2, 3, 0, 1, 4)).reshape(
+        2, heads, toks, 2 * hd
+    )
+    my_q = lax.dynamic_slice_in_dim(queries, me * here, here, 0).reshape(
+        here, kv_heads, group, hd
+    )
+    my_own = lax.dynamic_slice_in_dim(own_kv, me * here, here, 0)
+    own_score = jnp.sum(
+        my_q.astype(jnp.float32)
+        * my_own[:, 0].reshape(here, kv_heads, 1, hd).astype(jnp.float32),
+        axis=3,
+    ) * (scale * LOG2E)
+    own = jnp.transpose(own_score.reshape(here, 2, heads * group), (1, 0, 2))
+    own = jnp.pad(own, ((0, 0), (0, 0), (0, 128 - heads * group)))
+    own_v = my_own[:, 1].astype(jnp.float32)
+
+    vmem = pl.BlockSpec(memory_space=pltpu.VMEM)
+    hbm = pl.BlockSpec(memory_space=pl.ANY)
+    block = (group + 2) * here
+    return pl.pallas_call(
+        functools.partial(exchange_kernel, seq_total, heads, group, scale),
+        out_shape=(
+            jax.ShapeDtypeStruct((here, kv_heads * group * hd), jnp.bfloat16),
+            jax.ShapeDtypeStruct((here, kv_heads * group * n_sel), jnp.float32),
+        ),
+        in_specs=[vmem] * 6 + [hbm] * 2,
+        out_specs=(vmem, vmem),
+        scratch_shapes=[
+            pltpu.VMEM((rows, heads * group * hd), jnp.bfloat16),
+            pltpu.VMEM((heads, toks, 2 * hd), jnp.bfloat16),
+            pltpu.VMEM((heads, toks, 2 * hd), jnp.bfloat16),
+            pltpu.VMEM((8, rows), jnp.int32),
+            pltpu.VMEM((hd, 2 * toks), jnp.bfloat16),
+            pltpu.VMEM((2, 2 * toks, rows), jnp.float32),
+            pltpu.VMEM((2, 2 * toks, rows), jnp.bfloat16),
+            pltpu.VMEM((2 * toks, rows), jnp.float32),
+            pltpu.VMEM((group, 2 * page_dev, rows), jnp.float32),
+            pltpu.VMEM((128, rows), jnp.float32),
+            pltpu.VMEM((128, rows), jnp.float32),
+            pltpu.VMEM((heads, n_dev, block, hd), jnp.bfloat16),
+            pltpu.VMEM((heads, n_dev, block, hd), jnp.bfloat16),
+            pltpu.VMEM((n_dev, 2 * here, 128), jnp.float32),
+            pltpu.VMEM((n_dev, 2 * here, 128), jnp.float32),
+            pltpu.SemaphoreType.DMA((2,)),
+            pltpu.SemaphoreType.DMA((heads + 1,)),
+            pltpu.SemaphoreType.DMA((heads + 1,)),
+            pltpu.SemaphoreType.DMA((heads + 1, n_dev)),
+            pltpu.SemaphoreType.DMA((heads + 1, n_dev)),
+        ],
+        compiler_params=pltpu.CompilerParams(
+            collective_id=0, has_side_effects=True, vmem_limit_bytes=40 * 1024 * 1024
+        ),
+    )(ids, lengths.reshape(1, rows), pos, sel, own, own_v, queries, kv)
+
+
+def choose(token_kv, positions, page_owner, queries, own_kv, selected, lengths):
+    rows_here = queries.shape[0] // (2 * lax.axis_size("seq"))
+    run = direct_body if rows_here == 8 else body
+    return run(token_kv, positions, page_owner, queries, own_kv, selected, lengths)
+
+
 def solution(mesh):
     in_specs = (
         P("role", ("groups", "seq"), None, None),
@@ -204,4 +601,4 @@
         P("groups"),
     )
     out_specs = (P(("groups", "role", "seq"), None), P(("groups", "role", "seq"), None))
-    return jax.shard_map(body, mesh=mesh, in_specs=in_specs, out_specs=out_specs, check_vma=False)
+    return jax.shard_map(choose, mesh=mesh, in_specs=in_specs, out_specs=out_specs, check_vma=False)

time: 776 us -> 67.5 us (0.09)
  blocking collectives: 332 us -> 0 us
  local copies, waits for them, and re-layouts: 207 us -> 16 us
  matrix products: 127 us -> 0 us
  other arithmetic: 71.8 us -> 1.82 us
  Pallas kernels: 0 us -> 48.6 us
  between operations: 15 us -> 0.74 us
  waiting for transfers between devices: 8.25 us -> 0 us
  starting transfers between devices: 8.24 us -> 0 us
    all_to_all x3 -> x0, blocking collectives: 215 us -> none  [the longest x1 190 us: body(): lax.all_to_all(out_kv, 'seq', split_axis=0, concat_axis=0, tiled=True)]
    dot_general x163 -> x0, matrix products: 127 us -> none  [the longest x32 42.8 us: one_block(): jnp.einsum('rgt,td->rgd', weights.astype(jnp.bfloat16), value_rows, prefe...]
    dynamic_update_slice x88 -> x0, local copies, waits for them, and re-layouts: 74.1 us -> none  [the longest x56 54.4 us: attend(): lax.map(one_head, (key_heads, value_heads, summary_heads, query_heads, ch...]
    unnamed x1 -> x0, blocking collectives: 58.6 us -> none
    pmax x1 -> x0, blocking collectives: 58.3 us -> none  [body(): overall = lax.pmax(largest, ('role', 'seq'))]
    pallas_call x0 -> x1, Pallas kernels: none -> 48.6 us  [direct_body(): pl.pallas_call(functools.partial(exchange_kernel, seq_total, heads, group...]
    reduce_sum x33 -> x1, other arithmetic: 25.3 us -> 0.14 us  [direct_body(): jnp.sum(my_q.astype(jnp.float32) * my_own[:, 0].reshape(here, kv_heads, 1...]
    slice x2, local copies, waits for them, and re-layouts: 23.6 us -> 2.06 us  [the longest x1 1.17 us: direct_body(): pos = jnp.broadcast_to(positions[:, 0:1], (8, rows))]
  transfers between devices with their start and end apart: 5 -> 0, of which waited for: 1 -> 0; matrix products, arithmetic and copies ran while one was open for 4% -> 0% of each run, Pallas kernels for 0% -> 0%
where the time goes in v1:
time: 67.5 us; the launch traced here: 67.1 us
  Pallas kernels  48.6 us (72%)
  local copies, waits for them, and re-layouts  16 us (24%)
  other arithmetic  1.82 us (3%)
  between operations  0.74 us (1%)
    pallas_call x1, Pallas kernels, direct_body(): pl.pallas_call(functools.partial(exchange_kernel, seq_total, heads, group...  48.6 us
    another operation x2, local copies, waits for them, and re-layouts, direct_body(): token_kv[0].reshape(toks, 2, 2, heads, hd)  6.12 us
    reshape x1, local copies, waits for them, and re-layouts, direct_body(): jnp.transpose(token_kv[0].reshape(toks, 2, 2, heads, hd), (2, 3, 0, 1, 4))  3.19 us
    unnamed x8, local copies, waits for them, and re-layouts  2.88 us

profile of v1, /device:TPU:0, one launch (start us, length us, event | category | flops | bytes accessed | tf_op | source)
XLA Modules:
  0.0 67.1 jit_solution(6045880691030182293)
XLA Ops:
  0.6 0.9 %constant_dynamic-slice_fusion.1 = (bf16[8,1,1024]{2,1,0:T(2,128)(2,1)S(1)}, bf16[8,1,1024]{2,1,0:T(2,128)(2,1)S(1)}) fusion(bf16[128,2,1024]{2,1,0:T(2,128)(2,1)} %param.11, s32[]{:T(128)S(6)} %select_n.18, s32[]{:T(128)S(6)} %add.40), kind=kLoop, calls=%fused_computation.13 | loop fusion | bytes 65544 | tf_op jit(solution)/shard_map/slice | solution.py:546
  1.6 0.9 %constant_dynamic-slice_fusion.2 = bf16[8,8192]{1,0:T(8,128)(2,1)S(1)} fusion(bf16[128,8192]{1,0:T(8,128)(2,1)} %q_hbm.1, s32[]{:T(128)S(6)} %select_n.18), kind=kLoop, calls=%fused_computation.14 | loop fusion | bytes 262148 | tf_op jit(solution)/shard_map/dynamic_slice | solution.py:535
  2.5 0.1 fusion
  2.6 0.1 copy.20
  2.7 0.9 %convert_reduce_fusion = s32[32]{0:T(128)S(1)} fusion(s32[32]{0:T(128)} %param.9), kind=kLoop, calls=%fused_computation.8 | loop fusion | flops 5088 | bytes 256 | tf_op jit(solution)/shard_map/reduce_sum | solution.py:26
  3.6 0.7 iota_add_fusion
  4.3 0.1 broadcast_select_fusion
  4.4 0.1 broadcast_in_dim.6.ids_ref
  4.5 3.2 %reshape_squeeze.4 = bf16[512,2,2,4,128]{4,3,2,1,0:T(4,128)(2,1)S(1)} reshape(bf16[1,512,2,1024]{3,2,1,0:T(2,128)(2,1)} %param.7) | data formatting | bytes 4194304 | tf_op jit(solution)/shard_map/reshape;squeeze | solution.py:532
  7.6 3.0 %copy.34 = bf16[512,2,2,4,128]{4,1,0,3,2:T(2,128)(2,1)} copy(bf16[512,2,2,4,128]{4,3,2,1,0:T(4,128)(2,1)S(1)} %reshape_squeeze.4) | data formatting | bytes 4194304 | tf_op jit(solution)/shard_map/reshape;squeeze | solution.py:532
  10.6 0.0 copy-start.1
  10.6 0.0 copy-start.2
  10.6 3.2 %reshape.57.kv_hbm = bf16[2,4,512,256]{3,2,1,0:T(8,128)(2,1)S(1)} reshape(bf16[2,4,512,2,128]{4,3,2,1,0:T(2,128)(2,1)} %bitcast.22) | data formatting | bytes 4194304 | tf_op jit(solution)/shard_map/reshape | solution.py:532
  13.8 1.2 %slice.9 = s32[1,1]{1,0:T(1,128)} slice(s32[1,512]{1,0:T(1,128)} %param.8), slice={[0:1], [0:1]} | slice | bytes 8 | tf_op jit(solution)/shard_map/slice | solution.py:530
  15.0 0.6 broadcast_in_dim.8.pos_ref
  15.6 0.0 copy-done.1
  15.6 0.0 copy-done.2
  15.6 0.0 copy-start
  15.6 1.6 %copy-done = bf16[128,8192]{1,0:T(8,128)(2,1)S(1)} copy-done((bf16[128,8192]{1,0:T(8,128)(2,1)S(1)}, bf16[128,8192]{1,0:T(8,128)(2,1)}, u32[]{:S(2)}) %copy-start) | copy-done | bytes 2097176
  17.2 48.6 %shard_map.86 = (bf16[8,8192]{1,0:T(8,128)(2,1)S(1)}, f32[8,2048]{1,0:T(8,128)S(1)}) custom-call(s32[64,128]{1,0:T(8,128)S(1)} %broadcast_in_dim.6.ids_ref, s32[1,128]{1,0:T(1,128)S(1)} %bitcast.21, s32[8,128]{1,0:T(8,128)S(1)} %broadcast_in_dim.8.pos_ref, s32[8,32,128]{2,1,0:T(8,128)S(1)} %bitcast.20, f32[2,8,128]{2,1,0:T(8,128)S(1)} %pad.4.own_ref, ...), custom_call_target="tpu_custom_call" | custom-call | tf_op jit(solution)/shard_map/pallas_call | solution.py:551
  65.8 0.7 copy.37
  66.5 0.6 copy.38
  (4 shorter events, 0.0 us)
Async XLA Ops:
  10.6 5.0 %copy-start.1 = (s32[128,8,32]{0,2,1:T(8,128)S(1)}, s32[128,8,32]{0,2,1:T(8,128)}, u32[]{:S(2)}) copy-start(s32[128,8,32]{0,2,1:T(8,128)} %param.12) | copy-start | bytes 393220
  10.6 5.0 %copy-start.2 = (s32[128]{0:T(128)S(1)}, s32[128]{0:T(128)}, u32[]{:S(2)}) copy-start(s32[128]{0:T(128)} %param.13) | copy-start | bytes 1540
  15.6 1.6 %copy-start = (bf16[128,8192]{1,0:T(8,128)(2,1)S(1)}, bf16[128,8192]{1,0:T(8,128)(2,1)}, u32[]{:S(2)}) copy-start(bf16[128,8192]{1,0:T(8,128)(2,1)} %q_hbm.1) | copy-start | bytes 6291460

commit v2 on v0

--- a/solution.py
+++ b/solution.py
@@ -1,11 +1,16 @@
+import functools
 import math
 
 import jax
 import jax.numpy as jnp
 from jax import lax
+from jax.experimental import pallas as pl
+from jax.experimental.pallas import tpu as pltpu
 from jax.sharding import PartitionSpec as P
 
 NEG = -1e30
+LOG2E = 1.4426950408889634
+MESH = pl.DeviceIdType.MESH
 
 
 def from_behind(block, axis, distance):
@@ -193,6 +198,516 @@
     return (attended.reshape(rows_here, -1).astype(jnp.bfloat16), bounds.reshape(rows_here, -1))
 
 
+def exchange_kernel(
+    n_seq,
+    heads,
+    group,
+    scale,
+    slot_count,
+    col_ref,
+    row_ref,
+    lens_ref,
+    pos_ref,
+    sel_ref,
+    ownk_ref,
+    ownv_ref,
+    q_hbm,
+    kv_hbm,
+    att_ref,
+    bnd_ref,
+    q_buf,
+    q_mine,
+    kv_own,
+    kv_got,
+    pos_got,
+    ids_buf,
+    vt_buf,
+    s_buf,
+    p_buf,
+    bias_buf,
+    u_buf,
+    mt_buf,
+    keep_buf,
+    keep_ml,
+    y_send,
+    y_recv,
+    yml_send,
+    yml_recv,
+    z_send,
+    z_recv,
+    ml_send,
+    ml_recv,
+    load_sem,
+    kv_ssem,
+    kv_rsem,
+    y_ssem,
+    y_rsem,
+    z_ssem,
+    z_rsem,
+):
+    role = lax.axis_index("role")
+    seq = lax.axis_index("seq")
+    y = seq % 2
+    z = seq // 2
+    n_z = n_seq // 2
+    n_same = 2 * n_z
+    me = role * n_z + z
+    mate = {"role": 1 - role, "seq": seq}
+    beside = {"role": role, "seq": z * 2 + 1 - y}
+    toks = kv_own.shape[2]
+    hd = kv_own.shape[3]
+    pages = toks // 16
+    rows = q_buf.shape[0]
+    here = rows // (2 * n_seq)
+    half = q_buf.shape[1]
+    pairs = group // 2
+    n_sel = sel_ref.shape[1]
+
+    def place_of(t):
+        return {"role": t // n_z, "seq": (t % n_z) * 2 + y}
+
+    q_copy = pltpu.make_async_copy(
+        q_hbm.at[:, pl.ds(pl.multiple_of(role * half, half), half)], q_buf, load_sem.at[0]
+    )
+    q_copy.start()
+    mine_at = pl.multiple_of(me * 2 * here, 2 * here)
+    mine_copy = pltpu.make_async_copy(
+        q_hbm.at[pl.ds(mine_at, 2 * here), :], q_mine, load_sem.at[1]
+    )
+    mine_copy.start()
+
+    def own_copy(hl):
+        at = pl.multiple_of((role * heads + hl) * hd, hd)
+        return pltpu.make_async_copy(
+            kv_hbm.at[:, :, pl.ds(at, hd)], kv_own.at[hl], load_sem.at[2 + hl]
+        )
+
+    for hl in range(heads):
+        own_copy(hl).start()
+
+    barrier = pltpu.get_barrier_semaphore()
+
+    def greet(j, carry):
+        t = lax.rem(me + j, n_same)
+        pl.semaphore_signal(barrier, inc=1, device_id=place_of(t), device_id_type=MESH)
+        return carry
+
+    lax.fori_loop(1, n_same, greet, 0)
+    pl.semaphore_signal(barrier, inc=1, device_id=beside, device_id_type=MESH)
+    pl.semaphore_wait(barrier, n_same)
+
+    def mate_copy(hl):
+        at = pl.multiple_of(((1 - role) * heads + hl) * hd, hd)
+        return pltpu.make_async_remote_copy(
+            src_ref=kv_hbm.at[:, :, pl.ds(at, hd)],
+            dst_ref=kv_got.at[hl],
+            send_sem=kv_ssem.at[hl],
+            recv_sem=kv_rsem.at[hl],
+            device_id=mate,
+            device_id_type=MESH,
+        )
+
+    pos_copy = pltpu.make_async_remote_copy(
+        src_ref=pos_ref,
+        dst_ref=pos_got,
+        send_sem=kv_ssem.at[heads],
+        recv_sem=kv_rsem.at[heads],
+        device_id=mate,
+        device_id_type=MESH,
+    )
+    pos_copy.start()
+    for hl in range(heads):
+        mate_copy(hl).start()
+
+    col = col_ref[...]
+    earlier = lax.broadcasted_iota(jnp.int32, (pages, pages), 1) < lax.broadcasted_iota(
+        jnp.int32, (pages, pages), 0
+    )
+    same = (col[:, 0:pages] == row_ref[...]) & earlier
+    rank = jnp.sum(jnp.where(same, 1.0, 0.0), axis=1, keepdims=True).astype(jnp.int32)
+    inbound = n_seq * slot_count
+    pool_dev = inbound + pages
+    new_ids = col * pool_dev + seq * slot_count + rank
+    old_ids = (
+        lax.broadcasted_iota(jnp.int32, (pages, rows), 0) + seq * pool_dev + inbound
+    )
+    ids_buf[0:pages, :] = jnp.where(role == 0, new_ids, old_ids)
+    ids_buf[pages : 2 * pages, :] = jnp.where(role == 0, old_ids, new_ids)
+    mt_buf[...] = jnp.zeros_like(mt_buf)
+    q_copy.wait()
+    pos_copy.wait()
+
+    def y_copy(hl):
+        return pltpu.make_async_remote_copy(
+            src_ref=y_send.at[hl],
+            dst_ref=y_recv.at[hl],
+            send_sem=y_ssem.at[0, hl],
+            recv_sem=y_rsem.at[0, hl],
+            device_id=beside,
+            device_id_type=MESH,
+        )
+
+    def yml_copy(hl):
+        return pltpu.make_async_remote_copy(
+            src_ref=yml_send.at[hl],
+            dst_ref=yml_recv.at[hl],
+            send_sem=y_ssem.at[1, hl],
+            recv_sem=y_rsem.at[1, hl],
+            device_id=beside,
+            device_id_type=MESH,
+        )
+
+    def z_copy(hl, t, slot):
+        return pltpu.make_async_remote_copy(
+            src_ref=z_send.at[hl, t],
+            dst_ref=z_recv.at[hl, slot],
+            send_sem=z_ssem.at[hl, t],
+            recv_sem=z_rsem.at[hl, slot],
+            device_id=place_of(t),
+            device_id_type=MESH,
+        )
+
+    def ml_copy(t, slot):
+        return pltpu.make_async_remote_copy(
+            src_ref=ml_send.at[t],
+            dst_ref=ml_recv.at[slot],
+            send_sem=z_ssem.at[heads, t],
+            recv_sem=z_rsem.at[heads, slot],
+            device_id=place_of(t),
+            device_id_type=MESH,
+        )
+
+    def split(first, second):
+        count = first.shape[0]
+        low = (lax.broadcasted_iota(jnp.int32, (count, rows), 1) // here) % 2 == 0
+        zero = jnp.where(low, first, pltpu.roll(second, here, 1))
+        one = jnp.where(low, pltpu.roll(first, rows - here, 1), second)
+        return jnp.where(y == 0, zero, one), jnp.where(y == 0, one, zero)
+
+    lens = lens_ref[...]
+    dims = (((1,), (1,)), ((), ()))
+
+    def merge(hl):
+        y_copy(hl).wait()
+        yml_copy(hl).wait()
+        for gp in range(pairs):
+            m1 = keep_ml[hl, gp : gp + 1, :]
+            l1 = keep_ml[hl, pairs + gp : pairs + gp + 1, :]
+            m2 = yml_recv[hl, gp : gp + 1, :]
+            l2 = yml_recv[hl, pairs + gp : pairs + gp + 1, :]
+            top = jnp.maximum(m1, m2)
+            w1 = jnp.exp2(m1 - top) * l1
+            w2 = jnp.exp2(m2 - top) * l2
+            total = w1 + w2
+            inv = 1.0 / total
+            o = keep_buf[hl, gp, 0:hd, :] * (w1 * inv) + y_recv[hl, gp, 0:hd, :].astype(
+                jnp.float32
+            ) * (w2 * inv)
+            z_send[hl, :, gp * 2 * here : (gp + 1) * 2 * here, :] = (
+                o.T.reshape(n_same, 2 * here, hd).astype(jnp.bfloat16)
+            )
+            mt_buf[pl.ds(hl * pairs + gp, 1), :] = top
+            mt_buf[pl.ds(64 + hl * pairs + gp, 1), :] = total
+        bound = jnp.concatenate(
+            [
+                keep_buf[hl, gp, hd : hd + n_sel, :]
+                + y_recv[hl, gp, hd : hd + n_sel, :].astype(jnp.float32)
+                for gp in range(pairs)
+            ],
+            axis=0,
+        )
+        z_send[hl, :, group * here : (group + 2) * here, :] = (
+            bound.T.reshape(n_same, 2 * here, hd).astype(jnp.bfloat16)
+        )
+
+        def go(j, carry):
+            z_copy(hl, lax.rem(me + j, n_same), me).start()
+            return carry
+
+        lax.fori_loop(1, n_same, go, 0)
+        z_recv[hl, me] = z_send[hl, me]
+
+    def one_head(hl, carry):
+        own_copy(hl).wait()
+        mate_copy(hl).wait()
+        sel = sel_ref[role * heads + hl]
+        ids = ids_buf[...]
+        hit = jnp.zeros((2 * pages, rows), jnp.float32) + NEG
+        for s in range(n_sel):
+            hit = jnp.where(ids == sel[s : s + 1, :], 0.0, hit)
+        tops = []
+        lows = []
+        for part in range(2):
+            start = (pos_ref if part == 0 else pos_got)[0:1, 0:1]
+            left = lens - start
+            wide = jnp.broadcast_to(
+                hit[part * pages : (part + 1) * pages][:, None, :], (pages, 16, rows)
+            ).reshape(toks, rows)
+            place = lax.broadcasted_iota(jnp.int32, (toks, rows), 0)
+            bias_buf[part * toks : (part + 1) * toks, :] = jnp.where(place < left, wide, NEG)
+            block = kv_own if part == 0 else kv_got
+            k32 = block[hl, 0].astype(jnp.float32).reshape(pages, 16, hd)
+            tops.append(jnp.max(k32, axis=1))
+            lows.append(jnp.min(k32, axis=1))
+            v32 = block[hl, 1].astype(jnp.float32)
+            vt_buf[:, part * toks : (part + 1) * toks] = v32.T.astype(jnp.bfloat16)
+        summary = jnp.concatenate(
+            [jnp.concatenate(tops, axis=0), jnp.concatenate(lows, axis=0)], axis=1
+        ).astype(jnp.bfloat16)
+
+        def one_pair(gp, carry):
+            at = (hl * group + gp * 2) * hd
+            q = jnp.concatenate(
+                [
+                    q_buf[:, pl.ds(pl.multiple_of(at, hd), hd)],
+                    q_buf[:, pl.ds(pl.multiple_of(at + hd, hd), hd)],
+                ],
+                axis=0,
+            )
+            q32 = q.astype(jnp.float32)
+            signed = jnp.concatenate(
+                [jnp.maximum(q32, 0.0), jnp.minimum(q32, 0.0)], axis=1
+            ).astype(jnp.bfloat16)
+            u_buf[gp] = (
+                lax.dot_general(summary, signed, dims, preferred_element_type=jnp.float32) * scale
+            )
+            for part in range(2):
+                block = kv_own if part == 0 else kv_got
+                bias = bias_buf[part * toks : (part + 1) * toks, :]
+                s_buf[part * toks : (part + 1) * toks, :] = lax.dot_general(
+                    block[hl, 0], q, dims, preferred_element_type=jnp.float32
+                ) * (scale * LOG2E) + jnp.concatenate([bias, bias], axis=1)
+            top = jnp.max(s_buf[...], axis=0, keepdims=True)
+            w = jnp.exp2(s_buf[...] - top)
+            total = jnp.sum(w, axis=0, keepdims=True)
+            p_buf[...] = w.astype(jnp.bfloat16)
+            o = jnp.dot(vt_buf[...], p_buf[...], preferred_element_type=jnp.float32)
+            o = o * (1.0 / total)
+            kept, sent = split(o[:, 0:rows], o[:, rows : 2 * rows])
+            keep_buf[hl, gp, 0:hd, :] = kept
+            y_send[hl, gp, 0:hd, :] = sent.astype(jnp.bfloat16)
+            for stat, base in ((top, 0), (total, pairs)):
+                stat = jnp.broadcast_to(stat, (8, 2 * rows))
+                kept, sent = split(stat[:, 0:rows], stat[:, rows : 2 * rows])
+                keep_ml[hl, pl.ds(base + gp, 1), :] = kept[0:1]
+                yml_send[hl, pl.ds(base + gp, 1), :] = sent[0:1]
+            return carry
+
+        lax.fori_loop(0, pairs, one_pair, 0)
+
+        acc = [jnp.zeros((n_sel, rows), jnp.float32) for _ in range(group)]
+        for p in range(2 * pages):
+            match = sel == ids_buf[p : p + 1, :]
+            for g in range(group):
+                at = (g % 2) * rows
+                acc[g] = jnp.where(match, u_buf[g // 2, p : p + 1, at : at + rows], acc[g])
+        for gp in range(pairs):
+            kept, sent = split(acc[2 * gp], acc[2 * gp + 1])
+            keep_buf[hl, gp, hd : hd + n_sel, :] = kept
+            y_send[hl, gp, hd : hd + n_sel, :] = sent.astype(jnp.bfloat16)
+        yml_copy(hl).start()
+        y_copy(hl).start()
+
+        @pl.when(hl > 0)
+        def _():
+            merge(hl - 1)
+
+        return carry
+
+    lax.fori_loop(0, heads, one_head, 0)
+    merge(heads - 1)
+
+    ml_send[...] = mt_buf[...].T.reshape(n_same, 2 * here, rows)
+
+    def go_ml(j, carry):
+        ml_copy(lax.rem(me + j, n_same), me).start()
+        return carry
+
+    lax.fori_loop(1, n_same, go_ml, 0)
+    ml_recv[me] = ml_send[me]
+
+    mine_copy.wait()
+    lane = lax.broadcasted_iota(jnp.int32, (2 * here, rows), 1)
+    fresh_scores = []
+    for r in range(2):
+        scores = jnp.zeros((2 * here, rows), jnp.float32)
+        for hl in range(heads):
+            h = r * heads + hl
+            own_k = ownk_ref[:, h * hd : (h + 1) * hd]
+            for gp in range(pairs):
+                sums = []
+                for sub in range(2):
+                    at = (h * group + gp * 2 + sub) * hd
+                    both = q_mine[:, at : at + hd].astype(jnp.float32)
+                    one = jnp.where(y == 0, both[0:here], both[here : 2 * here])
+                    sums.append(jnp.sum(one * own_k, axis=1, keepdims=True))
+                scores = jnp.where(
+                    lane == hl * pairs + gp, jnp.concatenate(sums, axis=0), scores
+                )
+        fresh_scores.append(scores * (scale * LOG2E))
+
+    def end_ml(j, carry):
+        t = lax.rem(me + j, n_same)
+        ml_copy(t, t).wait()
+        return carry
+
+    lax.fori_loop(1, n_same, end_ml, 0)
+
+    shares = []
+    for r in range(2):
+        mine = fresh_scores[r]
+        stats = [ml_recv[r * n_z + c] for c in range(n_z)]
+        highest = mine
+        for m in stats:
+            highest = jnp.maximum(highest, m)
+        fresh = jnp.exp2(mine - highest)
+        parts = [jnp.exp2(m - highest) * pltpu.roll(m, 64, 1) for m in stats]
+        inv = fresh
+        for w in parts:
+            inv = inv + w
+        inv = 1.0 / inv
+        shares.append([w * inv for w in parts] + [fresh * inv])
+
+    span = lax.broadcasted_iota(jnp.int32, (here, rows), 1) // n_sel
+    for hl in range(heads):
+
+        def end(j, carry):
+            t = lax.rem(me + j, n_same)
+            z_copy(hl, t, t).wait()
+            return carry
+
+        lax.fori_loop(1, n_same, end, 0)
+        for r in range(2):
+            h = r * heads + hl
+            own_v = ownv_ref[:, h * hd : (h + 1) * hd]
+            own_v = jnp.concatenate([own_v, own_v], axis=0)
+            for gp in range(pairs):
+                j = hl * pairs + gp
+                total = shares[r][n_z][:, j : j + 1] * own_v
+                for c in range(n_z):
+                    block = z_recv[
+                        hl, r * n_z + c, gp * 2 * here : (gp + 1) * 2 * here, :
+                    ].astype(jnp.float32)
+                    total = total + shares[r][c][:, j : j + 1] * block
+                at = (h * group + gp * 2) * hd
+                att_ref[:, at : at + hd] = total[0:here].astype(jnp.bfloat16)
+                att_ref[:, at + hd : at + 2 * hd] = total[here : 2 * here].astype(jnp.bfloat16)
+            bound = jnp.zeros((2 * here, hd), jnp.float32)
+            for c in range(n_z):
+                bound = bound + z_recv[
+                    hl, r * n_z + c, group * here : (group + 2) * here, :
+                ].astype(jnp.float32)
+            a = bound[0:here]
+            b = bound[here : 2 * here]
+            at = h * group * n_sel
+            bnd_ref[:, at : at + hd] = jnp.where(
+                span == 0,
+                a,
+                jnp.where(
+                    span == 1,
+                    pltpu.roll(b, 32, 1),
+                    jnp.where(span == 2, pltpu.roll(a, 32, 1), pltpu.roll(b, 64, 1)),
+                ),
+            )
+            bnd_ref[:, at + hd : at + 2 * hd] = jnp.where(
+                span == 0,
+                pltpu.roll(a, 64, 1),
+                jnp.where(
+                    span == 1,
+                    pltpu.roll(b, 96, 1),
+                    jnp.where(span == 2, pltpu.roll(a, 96, 1), b),
+                ),
+            )
+
+
+def direct_body(token_kv, positions, page_owner, queries, own_kv, selected, lengths):
+    seq_total = lax.axis_size("seq")
+    me = lax.axis_index("role") * seq_total + lax.axis_index("seq")
+    page_dev = page_owner.shape[0]
+    toks = token_kv.shape[1]
+    kv_width = token_kv.shape[3]
+    rows, kv_heads, n_sel = selected.shape
+    hd = kv_width // kv_heads
+    group = queries.shape[1] // kv_width
+    heads = kv_heads // 2
+    pairs = group // 2
+    slot_count = max(2, 4 * page_dev // seq_total)
+    n_same = seq_total
+    here = rows // (2 * seq_total)
+
+    col = jnp.broadcast_to(page_owner[:, None], (page_dev, rows))
+    sel = jnp.transpose(selected, (1, 2, 0))
+    kv = jnp.transpose(token_kv[0], (1, 0, 2))
+    my_own = lax.dynamic_slice_in_dim(own_kv, me * here, here, 0).astype(jnp.float32)
+
+    vmem = pl.BlockSpec(memory_space=pltpu.VMEM)
+    hbm = pl.BlockSpec(memory_space=pl.ANY)
+    block = (group + 2) * here
+    f32 = jnp.float32
+    bf16 = jnp.bfloat16
+    return pl.pallas_call(
+        functools.partial(
+            exchange_kernel, seq_total, heads, group, 1.0 / math.sqrt(hd), slot_count
+        ),
+        out_shape=(
+            jax.ShapeDtypeStruct((here, kv_heads * group * hd), bf16),
+            jax.ShapeDtypeStruct((here, kv_heads * group * n_sel), f32),
+        ),
+        in_specs=[vmem] * 7 + [hbm] * 2,
+        out_specs=(vmem, vmem),
+        scratch_shapes=[
+            pltpu.VMEM((rows, heads * group * hd), bf16),
+            pltpu.VMEM((2 * here, kv_heads * group * hd), bf16),
+            pltpu.VMEM((heads, 2, toks, hd), bf16),
+            pltpu.VMEM((heads, 2, toks, hd), bf16),
+            pltpu.VMEM((1, toks), jnp.int32),
+            pltpu.VMEM((2 * page_dev, rows), jnp.int32),
+            pltpu.VMEM((hd, 2 * toks), bf16),
+            pltpu.VMEM((2 * toks, 2 * rows), f32),
+            pltpu.VMEM((2 * toks, 2 * rows), bf16),
+            pltpu.VMEM((2 * toks, rows), f32),
+            pltpu.VMEM((pairs, 2 * page_dev, 2 * rows), f32),
+            pltpu.VMEM((128, rows), f32),
+            pltpu.VMEM((heads, pairs, hd + n_sel, rows), f32),
+            pltpu.VMEM((heads, 2 * pairs, rows), f32),
+            pltpu.VMEM((heads, pairs, hd + n_sel, rows), bf16),
+            pltpu.VMEM((heads, pairs, hd + n_sel, rows), bf16),
+            pltpu.VMEM((heads, 2 * pairs, rows), f32),
+            pltpu.VMEM((heads, 2 * pairs, rows), f32),
+            pltpu.VMEM((heads, n_same, block, hd), bf16),
+            pltpu.VMEM((heads, n_same, block, hd), bf16),
+            pltpu.VMEM((n_same, 2 * here, rows), f32),
+            pltpu.VMEM((n_same, 2 * here, rows), f32),
+            pltpu.SemaphoreType.DMA((heads + 2,)),
+            pltpu.SemaphoreType.DMA((heads + 1,)),
+            pltpu.SemaphoreType.DMA((heads + 1,)),
+            pltpu.SemaphoreType.DMA((2, heads)),
+            pltpu.SemaphoreType.DMA((2, heads)),
+            pltpu.SemaphoreType.DMA((heads + 1, n_same)),
+            pltpu.SemaphoreType.DMA((heads + 1, n_same)),
+        ],
+        compiler_params=pltpu.CompilerParams(
+            collective_id=0, has_side_effects=True, vmem_limit_bytes=60 * 1024 * 1024
+        ),
+    )(
+        col,
+        page_owner.reshape(1, page_dev),
+        lengths.reshape(1, rows),
+        positions,
+        sel,
+        my_own[:, 0],
+        my_own[:, 1],
+        queries,
+        kv,
+    )
+
+
+def choose(token_kv, positions, page_owner, queries, own_kv, selected, lengths):
+    rows_here = queries.shape[0] // (2 * lax.axis_size("seq"))
+    run = direct_body if rows_here == 8 else body
+    return run(token_kv, positions, page_owner, queries, own_kv, selected, lengths)
+
+
 def solution(mesh):
     in_specs = (
         P("role", ("groups", "seq"), None, None),
@@ -204,4 +719,4 @@
         P("groups"),
     )
     out_specs = (P(("groups", "role", "seq"), None), P(("groups", "role", "seq"), None))
-    return jax.shard_map(body, mesh=mesh, in_specs=in_specs, out_specs=out_specs, check_vma=False)
+    return jax.shard_map(choose, mesh=mesh, in_specs=in_specs, out_specs=out_specs, check_vma=False)

time: 776 us -> 50.9 us (0.07)
  blocking collectives: 332 us -> 0 us
  local copies, waits for them, and re-layouts: 207 us -> 8.63 us
  matrix products: 127 us -> 0 us
  other arithmetic: 71.8 us -> 0.01 us
  Pallas kernels: 0 us -> 41.3 us
  between operations: 15 us -> 0.67 us
  waiting for transfers between devices: 8.25 us -> 0 us
  starting transfers between devices: 8.24 us -> 0 us
    all_to_all x3 -> x0, blocking collectives: 215 us -> none  [the longest x1 190 us: body(): lax.all_to_all(out_kv, 'seq', split_axis=0, concat_axis=0, tiled=True)]
    dot_general x163 -> x0, matrix products: 127 us -> none  [the longest x32 42.8 us: one_block(): jnp.einsum('rgt,td->rgd', weights.astype(jnp.bfloat16), value_rows, prefe...]
    dynamic_update_slice x88 -> x0, local copies, waits for them, and re-layouts: 74.1 us -> none  [the longest x56 54.4 us: attend(): lax.map(one_head, (key_heads, value_heads, summary_heads, query_heads, ch...]
    unnamed x1 -> x0, blocking collectives: 58.6 us -> none
    pmax x1 -> x0, blocking collectives: 58.3 us -> none  [body(): overall = lax.pmax(largest, ('role', 'seq'))]
    pallas_call x0 -> x1, Pallas kernels: none -> 41.3 us  [direct_body(): pl.pallas_call(functools.partial(exchange_kernel, seq_total, heads, group...]
    reduce_sum x34 -> x0, other arithmetic: 26.2 us -> none  [the longest x32 25.2 us: one_block(): totals = jnp.sum(weights, axis=2)]
    slice x2 -> x0, local copies, waits for them, and re-layouts: 23.6 us -> none  [the longest x1 11.8 us: attend(): pool_kv[:, :, 0, :].reshape(token_total, kv_heads, head_dim)]
  transfers between devices with their start and end apart: 5 -> 0, of which waited for: 1 -> 0; matrix products, arithmetic and copies ran while one was open for 4% -> 0% of each run, Pallas kernels for 0% -> 0%
where the time goes in v2:
time: 50.9 us; the launch traced here: 50.6 us
  Pallas kernels  41.3 us (81%)
  local copies, waits for them, and re-layouts  8.63 us (17%)
  between operations  0.67 us (1%)
    pallas_call x1, Pallas kernels, direct_body(): pl.pallas_call(functools.partial(exchange_kernel, seq_total, heads, group...  41.3 us
    unnamed x5, local copies, waits for them, and re-layouts  6.59 us
    broadcast_in_dim x1, local copies, waits for them, and re-layouts, direct_body(): col = jnp.broadcast_to(page_owner[:, None], (page_dev, rows))  1.38 us

profile of v2, /device:TPU:0, one launch (start us, length us, event | category | flops | bytes accessed | tf_op | source)
XLA Modules:
  0.0 50.6 jit_solution(10821738960549522386)
XLA Ops:
  0.6 0.0 copy-start
  0.7 1.4 %broadcast_in_dim.2.col_ref = s32[32,128]{1,0:T(8,128)} broadcast(s32[32]{0:T(128)} %param.9), dimensions={0} | broadcast | bytes 16512 | tf_op jit(solution)/shard_map/broadcast_in_dim | solution.py:638
  2.0 0.0 copy-done
  2.1 0.6 %slice_bitcast_fusion = (f32[8,1024]{1,0:T(8,128)}, f32[8,1024]{1,0:T(8,128)}) fusion(f32[8,2,1024]{2,0,1:T(8,128)S(1)} %copy_convert_fusion), kind=kLoop, calls=%fused_computation.1 | loop fusion | bytes 131072 | tf_op jit(solution)/shard_map/squeeze | solution.py:699
  2.7 3.5 %copy.14 = bf16[1,512,2,1024]{3,1,2,0:T(8,128)(2,1)} copy(bf16[1,512,2,1024]{3,2,1,0:T(2,128)(2,1)} %param.7) | data formatting | bytes 4194304 | tf_op args[0]
  6.3 41.3 %shard_map.86 = (bf16[8,8192]{1,0:T(8,128)(2,1)}, f32[8,2048]{1,0:T(8,128)}) custom-call(s32[32,128]{1,0:T(8,128)} %broadcast_in_dim.2.col_ref, s32[1,32]{1,0:T(1,128)} %bitcast.14, s32[1,128]{1,0:T(1,128)} %bitcast.15, s32[1,512]{1,0:T(1,128)} %pos_ref.1, s32[8,32,128]{2,1,0:T(8,128)} %bitcast.13, f32[8,1024]{1,0:T(8,128)} %get-tuple-element.3.ownk_ref, ...), custom_call_target="tpu_custom_call" | custom-call | tf_op jit(solution)/shard_map/pallas_call | solution.py:648
  47.6 1.6 %copy.17 = bf16[8,8192]{1,0:T(8,128)(2,1)} copy(bf16[8,8192]{1,0:T(8,128)(2,1)} %get-tuple-element.6) | data formatting | bytes 262144
  49.2 1.5 %copy.18 = f32[8,2048]{1,0:T(8,128)} copy(f32[8,2048]{1,0:T(8,128)} %get-tuple-element.7) | data formatting | bytes 131072
  (2 shorter events, 0.0 us)
Async XLA Ops:
  0.6 1.4 %copy-start = (bf16[128,2,1024]{2,1,0:T(2,128)(2,1)S(1)}, bf16[128,2,1024]{2,1,0:T(2,128)(2,1)}, u32[]{:S(2)}) copy-start(bf16[128,2,1024]{2,1,0:T(2,128)(2,1)} %param.11) | copy-start | bytes 1572868

commit v3 on v2

--- a/solution.py
+++ b/solution.py
@@ -204,7 +204,6 @@
     group,
     scale,
     slot_count,
-    col_ref,
     row_ref,
     lens_ref,
     pos_ref,
@@ -319,11 +318,12 @@
     for hl in range(heads):
         mate_copy(hl).start()
 
-    col = col_ref[...]
-    earlier = lax.broadcasted_iota(jnp.int32, (pages, pages), 1) < lax.broadcasted_iota(
-        jnp.int32, (pages, pages), 0
-    )
-    same = (col[:, 0:pages] == row_ref[...]) & earlier
+    lanes = lax.broadcasted_iota(jnp.int32, (pages, pages), 1)
+    sublanes = lax.broadcasted_iota(jnp.int32, (pages, pages), 0)
+    owners = jnp.broadcast_to(row_ref[...].astype(jnp.float32), (pages, pages))
+    col = jnp.sum(jnp.where(lanes == sublanes, owners, 0.0), axis=1, keepdims=True)
+    same = (col == owners) & (lanes < sublanes)
+    col = jnp.broadcast_to(col, (pages, rows)).astype(jnp.int32)
     rank = jnp.sum(jnp.where(same, 1.0, 0.0), axis=1, keepdims=True).astype(jnp.int32)
     inbound = n_seq * slot_count
     pool_dev = inbound + pages
@@ -337,12 +337,12 @@
     q_copy.wait()
     pos_copy.wait()
 
-    def y_copy(hl):
+    def y_copy(hl, gp):
         return pltpu.make_async_remote_copy(
-            src_ref=y_send.at[hl],
-            dst_ref=y_recv.at[hl],
-            send_sem=y_ssem.at[0, hl],
-            recv_sem=y_rsem.at[0, hl],
+            src_ref=y_send.at[hl, gp],
+            dst_ref=y_recv.at[hl, gp],
+            send_sem=y_ssem.at[gp, hl],
+            recv_sem=y_rsem.at[gp, hl],
             device_id=beside,
             device_id_type=MESH,
         )
@@ -351,8 +351,8 @@
         return pltpu.make_async_remote_copy(
             src_ref=yml_send.at[hl],
             dst_ref=yml_recv.at[hl],
-            send_sem=y_ssem.at[1, hl],
-            recv_sem=y_rsem.at[1, hl],
+            send_sem=y_ssem.at[pairs, hl],
+            recv_sem=y_rsem.at[pairs, hl],
             device_id=beside,
             device_id_type=MESH,
         )
@@ -388,9 +388,9 @@
     dims = (((1,), (1,)), ((), ()))
 
     def merge(hl):
-        y_copy(hl).wait()
         yml_copy(hl).wait()
         for gp in range(pairs):
+            y_copy(hl, gp).wait()
             m1 = keep_ml[hl, gp : gp + 1, :]
             l1 = keep_ml[hl, pairs + gp : pairs + gp + 1, :]
             m2 = yml_recv[hl, gp : gp + 1, :]
@@ -455,46 +455,24 @@
             [jnp.concatenate(tops, axis=0), jnp.concatenate(lows, axis=0)], axis=1
         ).astype(jnp.bfloat16)
 
-        def one_pair(gp, carry):
+        def query(gp):
             at = (hl * group + gp * 2) * hd
-            q = jnp.concatenate(
+            return jnp.concatenate(
                 [
                     q_buf[:, pl.ds(pl.multiple_of(at, hd), hd)],
                     q_buf[:, pl.ds(pl.multiple_of(at + hd, hd), hd)],
                 ],
                 axis=0,
             )
-            q32 = q.astype(jnp.float32)
+
+        for gp in range(pairs):
+            q32 = query(gp).astype(jnp.float32)
             signed = jnp.concatenate(
                 [jnp.maximum(q32, 0.0), jnp.minimum(q32, 0.0)], axis=1
             ).astype(jnp.bfloat16)
             u_buf[gp] = (
                 lax.dot_general(summary, signed, dims, preferred_element_type=jnp.float32) * scale
             )
-            for part in range(2):
-                block = kv_own if part == 0 else kv_got
-                bias = bias_buf[part * toks : (part + 1) * toks, :]
-                s_buf[part * toks : (part + 1) * toks, :] = lax.dot_general(
-                    block[hl, 0], q, dims, preferred_element_type=jnp.float32
-                ) * (scale * LOG2E) + jnp.concatenate([bias, bias], axis=1)
-            top = jnp.max(s_buf[...], axis=0, keepdims=True)
-            w = jnp.exp2(s_buf[...] - top)
-            total = jnp.sum(w, axis=0, keepdims=True)
-            p_buf[...] = w.astype(jnp.bfloat16)
-            o = jnp.dot(vt_buf[...], p_buf[...], preferred_element_type=jnp.float32)
-            o = o * (1.0 / total)
-            kept, sent = split(o[:, 0:rows], o[:, rows : 2 * rows])
-            keep_buf[hl, gp, 0:hd, :] = kept
-            y_send[hl, gp, 0:hd, :] = sent.astype(jnp.bfloat16)
-            for stat, base in ((top, 0), (total, pairs)):
-                stat = jnp.broadcast_to(stat, (8, 2 * rows))
-                kept, sent = split(stat[:, 0:rows], stat[:, rows : 2 * rows])
-                keep_ml[hl, pl.ds(base + gp, 1), :] = kept[0:1]
-                yml_send[hl, pl.ds(base + gp, 1), :] = sent[0:1]
-            return carry
-
-        lax.fori_loop(0, pairs, one_pair, 0)
-
         acc = [jnp.zeros((n_sel, rows), jnp.float32) for _ in range(group)]
         for p in range(2 * pages):
             match = sel == ids_buf[p : p + 1, :]
@@ -505,13 +483,57 @@
             kept, sent = split(acc[2 * gp], acc[2 * gp + 1])
             keep_buf[hl, gp, hd : hd + n_sel, :] = kept
             y_send[hl, gp, hd : hd + n_sel, :] = sent.astype(jnp.bfloat16)
-        yml_copy(hl).start()
-        y_copy(hl).start()
 
         @pl.when(hl > 0)
         def _():
             merge(hl - 1)
 
+        step = toks // 2
+        chunks = 4
+
+        def score(gp):
+            q = query(gp)
+            top = None
+            for ch in range(chunks):
+                block = kv_own if ch < 2 else kv_got
+                first = (ch % 2) * step
+                bias = bias_buf[ch * step : (ch + 1) * step, :]
+                part = lax.dot_general(
+                    block[hl, 0, first : first + step, :],
+                    q,
+                    dims,
+                    preferred_element_type=jnp.float32,
+                ) * (scale * LOG2E) + jnp.concatenate([bias, bias], axis=1)
+                s_buf[gp % 2, ch * step : (ch + 1) * step, :] = part
+                high = jnp.max(part.reshape(step // 8, 8, 2 * rows), axis=0)
+                top = high if top is None else jnp.maximum(top, high)
+            return jnp.max(top, axis=0, keepdims=True)
+
+        def attend_pair(gp, top):
+            total = jnp.zeros((8, 2 * rows), jnp.float32)
+            for ch in range(chunks):
+                w = jnp.exp2(s_buf[gp % 2, ch * step : (ch + 1) * step, :] - top)
+                total = total + jnp.sum(w.reshape(step // 8, 8, 2 * rows), axis=0)
+                p_buf[gp % 2, ch * step : (ch + 1) * step, :] = w.astype(jnp.bfloat16)
+            total = jnp.sum(total, axis=0, keepdims=True)
+            o = jnp.dot(vt_buf[...], p_buf[gp % 2], preferred_element_type=jnp.float32)
+            o = o * (1.0 / total)
+            kept, sent = split(o[:, 0:rows], o[:, rows : 2 * rows])
+            keep_buf[hl, gp, 0:hd, :] = kept
+            y_send[hl, gp, 0:hd, :] = sent.astype(jnp.bfloat16)
+            for stat, base in ((top, 0), (total, pairs)):
+                stat = jnp.broadcast_to(stat, (8, 2 * rows))
+                kept, sent = split(stat[:, 0:rows], stat[:, rows : 2 * rows])
+                keep_ml[hl, base + gp : base + gp + 1, :] = kept[0:1]
+                yml_send[hl, base + gp : base + gp + 1, :] = sent[0:1]
+            y_copy(hl, gp).start()
+
+        top = score(0)
+        for gp in range(pairs):
+            later = score(gp + 1) if gp + 1 < pairs else None
+            attend_pair(gp, top)
+            top = later
+        yml_copy(hl).start()
         return carry
 
     lax.fori_loop(0, heads, one_head, 0)
@@ -635,7 +657,6 @@
     n_same = seq_total
     here = rows // (2 * seq_total)
 
-    col = jnp.broadcast_to(page_owner[:, None], (page_dev, rows))
     sel = jnp.transpose(selected, (1, 2, 0))
     kv = jnp.transpose(token_kv[0], (1, 0, 2))
     my_own = lax.dynamic_slice_in_dim(own_kv, me * here, here, 0).astype(jnp.float32)
@@ -653,7 +674,7 @@
             jax.ShapeDtypeStruct((here, kv_heads * group * hd), bf16),
             jax.ShapeDtypeStruct((here, kv_heads * group * n_sel), f32),
         ),
-        in_specs=[vmem] * 7 + [hbm] * 2,
+        in_specs=[vmem] * 6 + [hbm] * 2,
         out_specs=(vmem, vmem),
         scratch_shapes=[
             pltpu.VMEM((rows, heads * group * hd), bf16),
@@ -663,8 +684,8 @@
             pltpu.VMEM((1, toks), jnp.int32),
             pltpu.VMEM((2 * page_dev, rows), jnp.int32),
             pltpu.VMEM((hd, 2 * toks), bf16),
-            pltpu.VMEM((2 * toks, 2 * rows), f32),
-            pltpu.VMEM((2 * toks, 2 * rows), bf16),
+            pltpu.VMEM((2, 2 * toks, 2 * rows), f32),
+            pltpu.VMEM((2, 2 * toks, 2 * rows), bf16),
             pltpu.VMEM((2 * toks, rows), f32),
             pltpu.VMEM((pairs, 2 * page_dev, 2 * rows), f32),
             pltpu.VMEM((128, rows), f32),
@@ -681,16 +702,15 @@
             pltpu.SemaphoreType.DMA((heads + 2,)),
             pltpu.SemaphoreType.DMA((heads + 1,)),
             pltpu.SemaphoreType.DMA((heads + 1,)),
-            pltpu.SemaphoreType.DMA((2, heads)),
-            pltpu.SemaphoreType.DMA((2, heads)),
+            pltpu.SemaphoreType.DMA((pairs + 1, heads)),
+            pltpu.SemaphoreType.DMA((pairs + 1, heads)),
             pltpu.SemaphoreType.DMA((heads + 1, n_same)),
             pltpu.SemaphoreType.DMA((heads + 1, n_same)),
         ],
         compiler_params=pltpu.CompilerParams(
-            collective_id=0, has_side_effects=True, vmem_limit_bytes=60 * 1024 * 1024
+            collective_id=0, has_side_effects=True, vmem_limit_bytes=36 * 1024 * 1024
         ),
     )(
-        col,
         page_owner.reshape(1, page_dev),
         lengths.reshape(1, rows),
         positions,

time: 50.9 us -> 47.5 us (0.933)
  local copies, waits for them, and re-layouts: 8.63 us -> 4.73 us
    unnamed x5 -> x15, local copies, waits for them, and re-layouts: 6.59 us -> 4.7 us
    broadcast_in_dim x1 -> x0, local copies, waits for them, and re-layouts: 1.38 us -> none  [direct_body(): col = jnp.broadcast_to(page_owner[:, None], (page_dev, rows))]
    squeeze x1, local copies, waits for them, and re-layouts: 0.63 us -> 0.01 us  [direct_body(): my_own[:, 1]]
where the time goes in v3:
time: 47.5 us; the launch traced here: 47.3 us
  Pallas kernels  41.8 us (88%)
  local copies, waits for them, and re-layouts  4.73 us (10%)
  between operations  0.76 us (2%)
    pallas_call x1, Pallas kernels, direct_body(): pl.pallas_call(functools.partial(exchange_kernel, seq_total, heads, group...  41.8 us
    unnamed x15, local copies, waits for them, and re-layouts  4.7 us

profile of v3, /device:TPU:0, one launch (start us, length us, event | category | flops | bytes accessed | tf_op | source)
XLA Modules:
  0.0 47.3 jit_solution(10062957384680685562)
XLA Ops:
  0.6 0.0 copy-start
  0.7 1.0 %copy-done = bf16[128,2,1024]{2,1,0:T(2,128)(2,1)S(1)} copy-done((bf16[128,2,1024]{2,1,0:T(2,128)(2,1)S(1)}, bf16[128,2,1024]{2,1,0:T(2,128)(2,1)}, u32[]{:S(2)}) %copy-start) | copy-done | bytes 524312
  1.7 0.0 copy-start.1
  1.7 0.0 copy-start.2
  1.8 0.0 copy-start.3
  1.8 0.0 copy-start.4
  1.8 0.0 copy-start.5
  1.8 2.4 %copy.14 = bf16[1,512,2,1024]{3,1,2,0:T(8,128)(2,1)S(1)} copy(bf16[1,512,2,1024]{3,2,1,0:T(2,128)(2,1)} %param.7) | data formatting | bytes 4194304 | tf_op args[0]
  4.2 0.0 copy-done.1
  4.2 0.0 copy-done.2
  4.2 0.0 copy-done.3
  4.2 0.0 copy-done.4
  4.2 0.0 copy-done.5
  4.2 41.8 %shard_map.86 = (bf16[8,8192]{1,0:T(8,128)(2,1)S(1)}, f32[8,2048]{1,0:T(8,128)S(1)}) custom-call(s32[1,32]{1,0:T(1,128)S(1)} %bitcast.14, s32[1,128]{1,0:T(1,128)S(1)} %bitcast.15, s32[1,512]{1,0:T(1,128)S(1)} %copy-done.3, s32[8,32,128]{2,1,0:T(8,128)S(1)} %bitcast.13, f32[8,1024]{1,0:T(8,128)S(1)} %get-tuple-element.3.ownk_ref, ...), custom_call_target="tpu_custom_call" | custom-call | tf_op jit(solution)/shard_map/pallas_call | solution.py:669
  46.0 0.7 %copy.17 = bf16[8,8192]{1,0:T(8,128)(2,1)} copy(bf16[8,8192]{1,0:T(8,128)(2,1)S(1)} %get-tuple-element.6) | data formatting | bytes 262144
  46.7 0.6 %copy.18 = f32[8,2048]{1,0:T(8,128)} copy(f32[8,2048]{1,0:T(8,128)S(1)} %get-tuple-element.7) | data formatting | bytes 131072
  (3 shorter events, 0.0 us)
Async XLA Ops:
  0.6 1.0 %copy-start = (bf16[128,2,1024]{2,1,0:T(2,128)(2,1)S(1)}, bf16[128,2,1024]{2,1,0:T(2,128)(2,1)}, u32[]{:S(2)}) copy-start(bf16[128,2,1024]{2,1,0:T(2,128)(2,1)} %param.11) | copy-start | bytes 1572868
  1.7 2.4 %copy-start.1 = (bf16[128,8192]{1,0:T(8,128)(2,1)S(1)}, bf16[128,8192]{1,0:T(8,128)(2,1)}, u32[]{:S(2)}) copy-start(bf16[128,8192]{1,0:T(8,128)(2,1)} %q_hbm.1) | copy-start | bytes 6291460
  1.7 2.4 %copy-start.2 = (s32[128,8,32]{0,2,1:T(8,128)S(1)}, s32[128,8,32]{0,2,1:T(8,128)}, u32[]{:S(2)}) copy-start(s32[128,8,32]{0,2,1:T(8,128)} %param.12) | copy-start | bytes 393220
  1.8 2.4 %copy-start.3 = (s32[1,512]{1,0:T(1,128)S(1)}, s32[1,512]{1,0:T(1,128)}, u32[]{:S(2)}) copy-start(s32[1,512]{1,0:T(1,128)} %pos_ref.1) | copy-start | bytes 6148
  1.8 2.4 %copy-start.4 = (s32[32]{0:T(128)S(1)}, s32[32]{0:T(128)}, u32[]{:S(2)}) copy-start(s32[32]{0:T(128)} %param.9) | copy-start | bytes 388
  1.8 2.4 %copy-start.5 = (s32[128]{0:T(128)S(1)}, s32[128]{0:T(128)}, u32[]{:S(2)}) copy-start(s32[128]{0:T(128)} %param.13) | copy-start | bytes 1540

commit v4 on v3

--- a/solution.py
+++ b/solution.py
@@ -484,10 +484,6 @@
             keep_buf[hl, gp, hd : hd + n_sel, :] = kept
             y_send[hl, gp, hd : hd + n_sel, :] = sent.astype(jnp.bfloat16)
 
-        @pl.when(hl > 0)
-        def _():
-            merge(hl - 1)
-
         step = toks // 2
         chunks = 4
 
@@ -533,6 +529,12 @@
             later = score(gp + 1) if gp + 1 < pairs else None
             attend_pair(gp, top)
             top = later
+            if gp == pairs - 2:
+
+                @pl.when(hl > 0)
+                def _():
+                    merge(hl - 1)
+
         yml_copy(hl).start()
         return carry
 

time: 47.5 us -> 41.3 us (0.87)
  Pallas kernels: 41.8 us -> 35.6 us
    pallas_call x1, Pallas kernels: 41.8 us -> 35.6 us  [direct_body(): pl.pallas_call(functools.partial(exchange_kernel, seq_total, heads, group...]
where the time goes in v4:
time: 41.3 us; the launch traced here: 41.1 us
  Pallas kernels  35.6 us (86%)
  local copies, waits for them, and re-layouts  4.73 us (11%)
  between operations  0.76 us (2%)
    pallas_call x1, Pallas kernels, direct_body(): pl.pallas_call(functools.partial(exchange_kernel, seq_total, heads, group...  35.6 us
    unnamed x15, local copies, waits for them, and re-layouts  4.7 us

profile of v4, /device:TPU:0, one launch (start us, length us, event | category | flops | bytes accessed | tf_op | source)
XLA Modules:
  0.0 41.1 jit_solution(8691990302337165907)
XLA Ops:
  0.6 0.0 copy-start
  0.7 1.0 %copy-done = bf16[128,2,1024]{2,1,0:T(2,128)(2,1)S(1)} copy-done((bf16[128,2,1024]{2,1,0:T(2,128)(2,1)S(1)}, bf16[128,2,1024]{2,1,0:T(2,128)(2,1)}, u32[]{:S(2)}) %copy-start) | copy-done | bytes 524312
  1.7 0.0 copy-start.1
  1.7 0.0 copy-start.2
  1.8 0.0 copy-start.3
  1.8 0.0 copy-start.4
  1.8 0.0 copy-start.5
  1.8 2.4 %copy.14 = bf16[1,512,2,1024]{3,1,2,0:T(8,128)(2,1)S(1)} copy(bf16[1,512,2,1024]{3,2,1,0:T(2,128)(2,1)} %param.7) | data formatting | bytes 4194304 | tf_op args[0]
  4.2 0.0 copy-done.1
  4.2 0.0 copy-done.2
  4.2 0.0 copy-done.3
  4.2 0.0 copy-done.4
  4.2 0.0 copy-done.5
  4.2 35.6 %shard_map.86 = (bf16[8,8192]{1,0:T(8,128)(2,1)S(1)}, f32[8,2048]{1,0:T(8,128)S(1)}) custom-call(s32[1,32]{1,0:T(1,128)S(1)} %bitcast.14, s32[1,128]{1,0:T(1,128)S(1)} %bitcast.15, s32[1,512]{1,0:T(1,128)S(1)} %copy-done.3, s32[8,32,128]{2,1,0:T(8,128)S(1)} %bitcast.13, f32[8,1024]{1,0:T(8,128)S(1)} %get-tuple-element.3.ownk_ref, ...), custom_call_target="tpu_custom_call" | custom-call | tf_op jit(solution)/shard_map/pallas_call | solution.py:671
  39.9 0.7 %copy.17 = bf16[8,8192]{1,0:T(8,128)(2,1)} copy(bf16[8,8192]{1,0:T(8,128)(2,1)S(1)} %get-tuple-element.6) | data formatting | bytes 262144
  40.5 0.6 %copy.18 = f32[8,2048]{1,0:T(8,128)} copy(f32[8,2048]{1,0:T(8,128)S(1)} %get-tuple-element.7) | data formatting | bytes 131072
  (3 shorter events, 0.0 us)
Async XLA Ops:
  0.6 1.0 %copy-start = (bf16[128,2,1024]{2,1,0:T(2,128)(2,1)S(1)}, bf16[128,2,1024]{2,1,0:T(2,128)(2,1)}, u32[]{:S(2)}) copy-start(bf16[128,2,1024]{2,1,0:T(2,128)(2,1)} %param.11) | copy-start | bytes 1572868
  1.7 2.4 %copy-start.1 = (bf16[128,8192]{1,0:T(8,128)(2,1)S(1)}, bf16[128,8192]{1,0:T(8,128)(2,1)}, u32[]{:S(2)}) copy-start(bf16[128,8192]{1,0:T(8,128)(2,1)} %q_hbm.1) | copy-start | bytes 6291460
  1.7 2.4 %copy-start.2 = (s32[128,8,32]{0,2,1:T(8,128)S(1)}, s32[128,8,32]{0,2,1:T(8,128)}, u32[]{:S(2)}) copy-start(s32[128,8,32]{0,2,1:T(8,128)} %param.12) | copy-start | bytes 393220
  1.8 2.4 %copy-start.3 = (s32[1,512]{1,0:T(1,128)S(1)}, s32[1,512]{1,0:T(1,128)}, u32[]{:S(2)}) copy-start(s32[1,512]{1,0:T(1,128)} %pos_ref.1) | copy-start | bytes 6148
  1.8 2.4 %copy-start.4 = (s32[32]{0:T(128)S(1)}, s32[32]{0:T(128)}, u32[]{:S(2)}) copy-start(s32[32]{0:T(128)} %param.9) | copy-start | bytes 388
  1.8 2.4 %copy-start.5 = (s32[128]{0:T(128)S(1)}, s32[128]{0:T(128)}, u32[]{:S(2)}) copy-start(s32[128]{0:T(128)} %param.13) | copy-start | bytes 1540
